TPU v7x, 256 devices: a whole 4x4x8 slice. The times are simulated.
256 devices in a mesh: ctx: 32 (over z, x), head: 8 (over y, core).
Axes of the slice: x: 4, y: 4, z: 8, core: 2. Of those that a mesh axis runs over, the one named last changes fastest.
Arguments:
- cross_query: bfloat16 [16384, 3072], P('ctx', 'head'), may hold values from -130 to 130
- cross_grad: bfloat16 [16384, 3072], P('ctx', 'head'), may hold values from -6 to 6
- cache_keys: bfloat16 [16384, 1024], P(('ctx', 'head')), may hold values from -6 to 6
- cache_values: bfloat16 [16384, 1024], P(('ctx', 'head')), may hold values from -6 to 6
- retention_query: bfloat16 [16384, 3072], P('ctx', 'head'), may hold values from -3 to 3
- retention_key: bfloat16 [16384, 3072], P('ctx', 'head'), may hold values from -3 to 3
- retention_value: bfloat16 [16384, 3072], P('ctx', 'head'), may hold values from -6 to 6
- retention_grad: bfloat16 [16384, 3072], P('ctx', 'head'), may hold values from -0.59765625 to 0.59765625
- log_decay: float32 [24, 16384], P('head', 'ctx'), may hold values from -2 to 0
- doc_offsets: int32 [87], replicated, may hold values from 0 to 16384, as said below
Outputs:
- cross_query_grad: bfloat16 [16384, 3072], P('ctx', 'head')
- cache_keys_grad: bfloat16 [16384, 1024], P(('ctx', 'head'))
- cache_values_grad: bfloat16 [16384, 1024], P(('ctx', 'head'))
- retention_query_grad: bfloat16 [16384, 3072], P('ctx', 'head')
- retention_key_grad: bfloat16 [16384, 3072], P('ctx', 'head')
- retention_value_grad: bfloat16 [16384, 3072], P('ctx', 'head')
- decay_grad: float32 [24, 16384], P('head', 'ctx')
Inputs may be any that keep to these rules, and one draw needn't show every extreme that they name: doc_offsets[0] = 0; the entries never fall; document i holds positions doc_offsets[i] to doc_offsets[i+1] - 1; consecutive entries differ by at most 1536, by exactly 1536 at least once; the entries after the sequence's end equal 16384.
All inputs are finite; a program needn't handle non-finite values.
Results may differ from a plain program's by a relative error of at most 0.003.
The roundings to bfloat16 on the way count: a program that leaves them out, or rounds other values in their place, can miss the bound.
Values may be sent and summed in bfloat16 or wider, within the bound.
A program may use at most 128 MiB of HBM per device.

v0:
```python
import jax
import jax.numpy as jnp
from jax import lax
from jax.sharding import PartitionSpec as P

ATTENDER_NUMBER = 24
KV_HEADS = 8
DH = 128
DOC_DEVS = 3


def from_behind(block, axis, distance):
    devices = range(lax.axis_size(axis))
    route = [(i - distance, i) for i in devices if i - distance in devices]
    return lax.ppermute(block, axis, route)


def prefix(part, axis, combine, identity):
    count = lax.axis_size(axis)
    place = lax.axis_index(axis)
    ahead = count - 1 - place
    gathered = lax.all_gather(part, axis)
    state = jnp.zeros_like(part) + jnp.asarray(identity, part.dtype)

    def one(step, state):
        source = count - 1 - step
        return combine(state, lax.dynamic_index_in_dim(gathered, source, 0, False))

    return lax.fori_loop(0, ahead, one, state)


def doc_index(offsets, positions):
    return jnp.sum((offsets[None, :] <= positions[:, None]).astype(jnp.int32), axis=1) - 1


def block_summary(log_block, doc_block, before_doc):
    cum = jnp.cumsum(log_block, axis=1)
    final_doc = doc_block[-1]
    last_w = jnp.where((doc_block == final_doc)[None, :], jnp.exp(cum[:, -1:] - cum), 0.0)
    first_w = jnp.where((doc_block == before_doc)[None, :], jnp.exp(cum), 0.0)
    carried = jnp.where(final_doc == before_doc, jnp.exp(cum[:, -1]), 0.0)
    return (cum, last_w, first_w, carried)


def add_pair(earlier, later_one):
    return earlier + later_one


def on_device(
    cross_query,
    cross_grad,
    cache_keys,
    cache_values,
    retention_query,
    retention_key,
    retention_value,
    retention_grad,
    log_decay,
    doc_offsets,
):
    scaling = DH ** (-0.5)
    per_group = ATTENDER_NUMBER // KV_HEADS
    local_rows = cross_query.shape[0]
    my_rank = lax.axis_index("ctx")
    ctx_count = lax.axis_size("ctx")
    query_pos = my_rank * local_rows + jnp.arange(local_rows, dtype=jnp.int32)
    query_doc = doc_index(doc_offsets, query_pos)
    key_rows, value_rows = (
        lax.all_to_all(cache_keys, "head", split_axis=1, concat_axis=0, tiled=True),
        lax.all_to_all(cache_values, "head", split_axis=1, concat_axis=0, tiled=True),
    )
    kv_local = key_rows.shape[1] // DH
    queries = cross_query.reshape(local_rows, kv_local, per_group, DH)
    upstream = cross_grad.reshape(local_rows, kv_local, per_group, DH)
    arrived = [(key_rows, value_rows)]
    for distance in range(1, DOC_DEVS + 1):
        arrived.append(from_behind((key_rows, value_rows), "ctx", distance))
    prepared = []
    for distance in range(DOC_DEVS + 1):
        key_pos = (my_rank - distance) * local_rows + jnp.arange(local_rows, dtype=jnp.int32)
        key_doc = doc_index(doc_offsets, key_pos)
        allowed = (query_doc[:, None] == key_doc[None, :]) & (
            key_pos[None, :] <= query_pos[:, None]
        )
        live = key_doc[-1] >= query_doc[0]
        prepared.append(
            (
                arrived[distance][0].reshape(local_rows, kv_local, DH),
                arrived[distance][1].reshape(local_rows, kv_local, DH),
                allowed,
                live,
            )
        )

    def scores_of(item):
        return (
            jnp.einsum("tgad,kgd->gatk", queries, item[0], preferred_element_type=jnp.float32)
            * scaling
        )

    stats = (
        jnp.full((kv_local, per_group, local_rows), -1e30, jnp.float32),
        jnp.zeros((kv_local, per_group, local_rows), jnp.float32),
    )
    for item in prepared:
        stats_row_top, stats_row_sum = stats
        stats_masked = jnp.where(item[2], scores_of(item), -1e30)
        new_top = jnp.maximum(stats_row_top, jnp.max(stats_masked, axis=-1))
        terms = jnp.where(item[2], jnp.exp(stats_masked - new_top[..., None]), 0.0)
        stats = (
            new_top,
            stats_row_sum * jnp.exp(stats_row_top - new_top) + jnp.sum(terms, axis=-1),
        )
    row_top, row_sum = stats

    def weights_of(item):
        masked = jnp.where(item[2], scores_of(item), -1e30)
        exponent = jnp.where(item[2], jnp.exp(masked - row_top[..., None]), 0.0)
        return exponent / row_sum[..., None]

    attended = jnp.zeros((local_rows, kv_local, per_group, DH), jnp.float32)
    for item in prepared:
        output_weights_b = weights_of(item).astype(jnp.bfloat16)
        attended = attended + jnp.einsum(
            "gatk,kgd->tgad", output_weights_b, item[1], preferred_element_type=jnp.float32
        )
    row_dot = jnp.transpose(jnp.sum(upstream.astype(jnp.float32) * attended, axis=-1), (1, 2, 0))[
        ..., None
    ]
    zero_rows = jnp.zeros((local_rows, kv_local, DH), jnp.float32)
    query_total = jnp.zeros((local_rows, kv_local, per_group, DH), jnp.float32)
    key_sum = zero_rows
    value_sum = zero_rows
    for distance in range(DOC_DEVS + 1):
        grad_item = prepared[distance]
        grad_query_total = query_total
        weights = weights_of(grad_item)
        weights_b = weights.astype(jnp.bfloat16)
        dweights = jnp.einsum(
            "tgad,kgd->gatk", upstream, grad_item[1], preferred_element_type=jnp.float32
        )
        dscores_b = (weights * (dweights - row_dot)).astype(jnp.bfloat16)
        grad_query_total = grad_query_total + jnp.einsum(
            "gatk,kgd->tgad", dscores_b, grad_item[0], preferred_element_type=jnp.float32
        )
        key_part = (
            jnp.einsum("gatk,tgad->kgd", dscores_b, queries, preferred_element_type=jnp.float32)
            * scaling
        )
        value_part = jnp.einsum(
            "gatk,tgad->kgd", weights_b, upstream, preferred_element_type=jnp.float32
        )
        query_total, key_part, value_part = (grad_query_total, key_part, value_part)
        if distance == 0:
            key_sum = key_part
            value_sum = value_part
        else:
            key_back, value_back = from_behind((key_part, value_part), "ctx", -distance)
            key_sum = key_sum + key_back
            value_sum = value_sum + value_back
    cross_query_grad = (
        (query_total * scaling).astype(jnp.bfloat16).reshape(local_rows, kv_local * per_group * DH)
    )
    key_flat = key_sum.reshape(local_rows, kv_local * DH).astype(jnp.bfloat16)
    value_flat = value_sum.reshape(local_rows, kv_local * DH).astype(jnp.bfloat16)
    cache_keys_grad, cache_values_grad = (
        lax.all_to_all(key_flat, "head", split_axis=0, concat_axis=1, tiled=True),
        lax.all_to_all(value_flat, "head", split_axis=0, concat_axis=1, tiled=True),
    )
    heads_local = retention_query.shape[1] // DH
    query_rows = retention_query.reshape(local_rows, heads_local, DH)
    retained_keys = retention_key.reshape(local_rows, heads_local, DH)
    retained_values = retention_value.reshape(local_rows, heads_local, DH)
    retained_grad = retention_grad.reshape(local_rows, heads_local, DH)
    before_doc = doc_index(doc_offsets, jnp.reshape(my_rank * local_rows - 1, (1,)))[0]
    cum, last_w, first_w, carried = block_summary(log_decay, query_doc, before_doc)
    keys_w = (last_w.T[:, :, None] * retained_keys.astype(jnp.float32)).astype(jnp.bfloat16)
    queries_w = (scaling * first_w.T[:, :, None] * query_rows.astype(jnp.float32)).astype(
        jnp.bfloat16
    )
    own_state = jnp.einsum(
        "thd,the->hde", keys_w, retained_values, preferred_element_type=jnp.float32
    )
    own_grad = jnp.einsum(
        "thd,the->hde", queries_w, retained_grad, preferred_element_type=jnp.float32
    )
    zeros_state = jnp.zeros((heads_local, DH, DH), jnp.float32)
    zeros_head = jnp.zeros((heads_local,), jnp.float32)

    def relay_forward(turn, current):
        return from_behind(carried[:, None, None] * current + own_state, "ctx", 1)

    def relay_backward(turn, current):
        return from_behind(own_grad + carried[:, None, None] * current, "ctx", -1)

    state = lax.fori_loop(0, ctx_count - 1, relay_forward, zeros_state)
    later_grad = lax.fori_loop(0, ctx_count - 1, relay_backward, zeros_state)
    state_b = state.astype(jnp.bfloat16)
    later_b = later_grad.astype(jnp.bfloat16)
    positions = jnp.arange(local_rows, dtype=jnp.int32)
    same = (query_doc[:, None] == query_doc[None, :]) & (positions[None, :] <= positions[:, None])
    within = jnp.where(
        same[None], jnp.exp(jnp.minimum(cum[:, :, None] - cum[:, None, :], 0.0)), 0.0
    )
    grad_dots = jnp.einsum(
        "thd,shd->hts", retained_grad, retained_values, preferred_element_type=jnp.float32
    )
    query_dots = jnp.einsum(
        "thd,shd->hts", query_rows, retained_keys, preferred_element_type=jnp.float32
    )
    grad_w = (scaling * within * grad_dots).astype(jnp.bfloat16)
    score_w = (scaling * within * query_dots).astype(jnp.bfloat16)
    query_f = jnp.einsum(
        "hts,shd->thd", grad_w, retained_keys, preferred_element_type=jnp.float32
    ) + (scaling * first_w).T[:, :, None] * jnp.einsum(
        "the,hde->thd", retained_grad, state_b, preferred_element_type=jnp.float32
    )
    key_f = jnp.einsum(
        "hts,thd->shd", grad_w, query_rows, preferred_element_type=jnp.float32
    ) + last_w.T[:, :, None] * jnp.einsum(
        "she,hde->shd", retained_values, later_b, preferred_element_type=jnp.float32
    )
    value_f = jnp.einsum(
        "hts,the->she", score_w, retained_grad, preferred_element_type=jnp.float32
    ) + last_w.T[:, :, None] * jnp.einsum(
        "shd,hde->she", retained_keys, later_b, preferred_element_type=jnp.float32
    )
    residue = jnp.sum(query_rows.astype(jnp.float32) * query_f, axis=-1) - jnp.sum(
        retained_keys.astype(jnp.float32) * key_f, axis=-1
    )
    residue = residue.T
    suffix = jnp.flip(jnp.cumsum(jnp.flip(residue, 1), axis=1), 1)
    tail = prefix(suffix[:, 0], "ctx", add_pair, zeros_head)
    decay_grad = suffix + tail[:, None]
    return (
        cross_query_grad,
        cache_keys_grad,
        cache_values_grad,
        query_f.astype(jnp.bfloat16).reshape(local_rows, heads_local * DH),
        key_f.astype(jnp.bfloat16).reshape(local_rows, heads_local * DH),
        value_f.astype(jnp.bfloat16).reshape(local_rows, heads_local * DH),
        decay_grad,
    )


def solution(mesh):
    return jax.shard_map(
        on_device,
        mesh=mesh,
        in_specs=(
            P("ctx", "head"),
            P("ctx", "head"),
            P(("ctx", "head"), None),
            P(("ctx", "head"), None),
            P("ctx", "head"),
            P("ctx", "head"),
            P("ctx", "head"),
            P("ctx", "head"),
            P("head", "ctx"),
            P(),
        ),
        out_specs=(
            P("ctx", "head"),
            P(("ctx", "head"), None),
            P(("ctx", "head"), None),
            P("ctx", "head"),
            P("ctx", "head"),
            P("ctx", "head"),
            P("head", "ctx"),
        ),
        check_vma=False,
    )
```

profile of v0, /device:TPU:103, one launch (start us, length us, event | category | flops | bytes accessed | tf_op | source)
XLA Modules:
  0.0 923.0 jit_solution(6988991557780420473)
XLA Ops:
  27.6 320.7 %while.33 = (s32[]{:T(128)}, f32[3,128,128]{2,1,0:T(8,128)S(1)}, f32[3]{0:T(128)S(1)}, f32[3,128,128]{2,1,0:T(8,128)S(1)}, s32[]{:T(128)}) while((s32[]{:T(128)}, f32[3,128,128]{2,1,0:T(8,128)S(1)}, f32[3]{0:T(128)S(1)}, f32[3,128,128]{2,1,0:T(8,128)S(1)}, s32[]{:T(128)}) %tuple.86), condition=%wide.region_19.20_spmd, body=%wide.region_18.19_spmd.sunk | while | flops 98306 | bytes 1376369 | solution.py:197
  30.2 9.3 %collective-permute-done.1 = f32[3,128,128]{2,1,0:T(8,128)S(1)} collective-permute-done((f32[3,128,128]{2,1,0:T(8,128)S(1)}, f32[3,128,128]{2,1,0:T(8,128)S(1)}, u32[]{:S(2)}, u32[]{:S(2)}) %collective-permute-start.1) | collective-permute-done | bytes 196640 | tf_op jit(solution)/shard_map/while/body/eval_jaxpr/ppermute | solution.py:15
  41.5 8.9 collective-permute-done.1
  52.4 7.8 collective-permute-done.1
  62.2 7.8 collective-permute-done.1
  72.1 7.8 collective-permute-done.1
  81.9 7.8 collective-permute-done.1
  91.7 7.8 collective-permute-done.1
  101.5 7.8 collective-permute-done.1
  111.4 8.0 collective-permute-done.1
  121.4 9.1 collective-permute-done.1
  132.5 9.9 %collective-permute-done.1 = f32[3,128,128]{2,1,0:T(8,128)S(1)} collective-permute-done((f32[3,128,128]{2,1,0:T(8,128)S(1)}, f32[3,128,128]{2,1,0:T(8,128)S(1)}, u32[]{:S(2)}, u32[]{:S(2)}) %collective-permute-start.1) | collective-permute-done | bytes 196640 | tf_op jit(solution)/shard_map/while/body/eval_jaxpr/ppermute | solution.py:15
  144.4 9.0 collective-permute-done.1
  155.4 7.8 collective-permute-done.1
  165.2 7.8 collective-permute-done.1
  175.0 7.8 collective-permute-done.1
  184.9 7.8 collective-permute-done.1
  194.7 7.8 collective-permute-done.1
  204.5 7.8 collective-permute-done.1
  214.3 7.9 collective-permute-done.1
  224.3 9.0 collective-permute-done.1
  235.3 9.9 %collective-permute-done.1 = f32[3,128,128]{2,1,0:T(8,128)S(1)} collective-permute-done((f32[3,128,128]{2,1,0:T(8,128)S(1)}, f32[3,128,128]{2,1,0:T(8,128)S(1)}, u32[]{:S(2)}, u32[]{:S(2)}) %collective-permute-start.1) | collective-permute-done | bytes 196640 | tf_op jit(solution)/shard_map/while/body/eval_jaxpr/ppermute | solution.py:15
  247.3 9.1 collective-permute-done.1
  258.4 8.1 collective-permute-done.1
  268.5 7.8 collective-permute-done.1
  278.3 7.8 collective-permute-done.1
  288.2 7.8 collective-permute-done.1
  298.0 7.8 collective-permute-done.1
  307.8 7.8 collective-permute-done.1
  317.6 7.8 collective-permute-done.1
  327.5 8.8 collective-permute-done.1
  338.2 10.1 %collective-permute-done.1 = f32[3,128,128]{2,1,0:T(8,128)S(1)} collective-permute-done((f32[3,128,128]{2,1,0:T(8,128)S(1)}, f32[3,128,128]{2,1,0:T(8,128)S(1)}, u32[]{:S(2)}, u32[]{:S(2)}) %collective-permute-start.1) | collective-permute-done | bytes 196640 | tf_op jit(solution)/shard_map/while/body/eval_jaxpr/ppermute | solution.py:15
  354.3 313.1 %while.32 = (s32[]{:T(128)}, f32[3,128,128]{2,1,0:T(8,128)S(1)}, f32[3]{0:T(128)S(1)}, f32[3,128,128]{2,1,0:T(8,128)S(1)}, s32[]{:T(128)}) while((s32[]{:T(128)}, f32[3,128,128]{2,1,0:T(8,128)S(1)}, f32[3]{0:T(128)S(1)}, f32[3,128,128]{2,1,0:T(8,128)S(1)}, s32[]{:T(128)}) %tuple.92), condition=%wide.region_17.18_spmd, body=%wide.region_16.17_spmd.sunk | while | flops 98306 | bytes 1376369 | solution.py:196
  369.0 7.1 collective-permute-start
  398.5 7.1 collective-permute-start
  408.3 7.1 collective-permute-start
  438.7 7.1 collective-permute-start
  450.6 7.3 collective-permute-start
  461.8 7.4 collective-permute-start
  472.3 7.4 collective-permute-start
  482.4 7.1 collective-permute-start
  492.3 7.1 collective-permute-start
  521.7 7.1 collective-permute-start
  564.7 7.4 collective-permute-start
  575.1 7.4 collective-permute-start
  671.1 59.0 %all-reduce = f32[96]{0:T(128)S(1)} all-reduce(f32[96]{0:T(128)S(1)} %dynamic-update-slice), channel_id=2, replica_groups=mesh['ctx'=32,'head'=8] {'ctx'}, use_global_device_ids=true, to_apply=%add | all-reduce | flops 96 | bytes 768
  737.1 84.8 %all-to-all-start = ((bf16[64,8,128]{2,0,1:T(8,128)(2,1)}), bf16[64,8,128]{2,0,1:T(8,128)(2,1)S(1)}, u32[]{:S(2)}, u32[]{:S(2)}) async-start(bf16[64,8,128]{2,0,1:T(8,128)(2,1)} %copy_bitcast_fusion.3), calls=%async_computation | async-start | bytes 262144 | tf_op jit(solution)/shard_map/all_to_all | solution.py:69
  899.2 8.5 all-to-all-start.3
  (324 shorter events, 422.3 us)
Async XLA Ops:
  2.2 734.9 %all-to-all-start.1 = ((bf16[64,8,128]{2,0,1:T(8,128)(2,1)}), bf16[64,8,128]{2,0,1:T(8,128)(2,1)}, u32[]{:S(2)}, u32[]{:S(2)}) async-start(bf16[64,8,128]{2,0,1:T(8,128)(2,1)} %copy_bitcast_fusion.2), calls=%async_computation.1 | async-start | bytes 262144 | tf_op jit(solution)/shard_map/all_to_all | solution.py:70
  27.7 11.7 %collective-permute-start.1 = (f32[3,128,128]{2,1,0:T(8,128)S(1)}, f32[3,128,128]{2,1,0:T(8,128)S(1)}, u32[]{:S(2)}, u32[]{:S(2)}) collective-permute-start(f32[3,128,128]{2,1,0:T(8,128)S(1)} %multiply_add_fusion.6), channel_id=1, source_target_pairs={{8,0},{16,8},{24,16},{32,24},{40,32},{48,40},{56,48},{64,56},{72,6... | collective-permute-start | bytes 589832 | tf_op jit(solution)/shard_map/while/body/eval_jaxpr/ppermute | solution.py:15
  39.6 10.8 %collective-permute-start.1 = (f32[3,128,128]{2,1,0:T(8,128)S(1)}, f32[3,128,128]{2,1,0:T(8,128)S(1)}, u32[]{:S(2)}, u32[]{:S(2)}) collective-permute-start(f32[3,128,128]{2,1,0:T(8,128)S(1)} %multiply_add_fusion.6), channel_id=1, source_target_pairs={{8,0},{16,8},{24,16},{32,24},{40,32},{48,40},{56,48},{64,56},{72,6... | collective-permute-start | bytes 589832 | tf_op jit(solution)/shard_map/while/body/eval_jaxpr/ppermute | solution.py:15
  109.4 9.9 %collective-permute-start.1 = (f32[3,128,128]{2,1,0:T(8,128)S(1)}, f32[3,128,128]{2,1,0:T(8,128)S(1)}, u32[]{:S(2)}, u32[]{:S(2)}) collective-permute-start(f32[3,128,128]{2,1,0:T(8,128)S(1)} %multiply_add_fusion.6), channel_id=1, source_target_pairs={{8,0},{16,8},{24,16},{32,24},{40,32},{48,40},{56,48},{64,56},{72,6... | collective-permute-start | bytes 589832 | tf_op jit(solution)/shard_map/while/body/eval_jaxpr/ppermute | solution.py:15
  119.4 11.0 %collective-permute-start.1 = (f32[3,128,128]{2,1,0:T(8,128)S(1)}, f32[3,128,128]{2,1,0:T(8,128)S(1)}, u32[]{:S(2)}, u32[]{:S(2)}) collective-permute-start(f32[3,128,128]{2,1,0:T(8,128)S(1)} %multiply_add_fusion.6), channel_id=1, source_target_pairs={{8,0},{16,8},{24,16},{32,24},{40,32},{48,40},{56,48},{64,56},{72,6... | collective-permute-start | bytes 589832 | tf_op jit(solution)/shard_map/while/body/eval_jaxpr/ppermute | solution.py:15
  130.5 11.8 %collective-permute-start.1 = (f32[3,128,128]{2,1,0:T(8,128)S(1)}, f32[3,128,128]{2,1,0:T(8,128)S(1)}, u32[]{:S(2)}, u32[]{:S(2)}) collective-permute-start(f32[3,128,128]{2,1,0:T(8,128)S(1)} %multiply_add_fusion.6), channel_id=1, source_target_pairs={{8,0},{16,8},{24,16},{32,24},{40,32},{48,40},{56,48},{64,56},{72,6... | collective-permute-start | bytes 589832 | tf_op jit(solution)/shard_map/while/body/eval_jaxpr/ppermute | solution.py:15
  142.4 10.9 %collective-permute-start.1 = (f32[3,128,128]{2,1,0:T(8,128)S(1)}, f32[3,128,128]{2,1,0:T(8,128)S(1)}, u32[]{:S(2)}, u32[]{:S(2)}) collective-permute-start(f32[3,128,128]{2,1,0:T(8,128)S(1)} %multiply_add_fusion.6), channel_id=1, source_target_pairs={{8,0},{16,8},{24,16},{32,24},{40,32},{48,40},{56,48},{64,56},{72,6... | collective-permute-start | bytes 589832 | tf_op jit(solution)/shard_map/while/body/eval_jaxpr/ppermute | solution.py:15
  212.4 9.9 %collective-permute-start.1 = (f32[3,128,128]{2,1,0:T(8,128)S(1)}, f32[3,128,128]{2,1,0:T(8,128)S(1)}, u32[]{:S(2)}, u32[]{:S(2)}) collective-permute-start(f32[3,128,128]{2,1,0:T(8,128)S(1)} %multiply_add_fusion.6), channel_id=1, source_target_pairs={{8,0},{16,8},{24,16},{32,24},{40,32},{48,40},{56,48},{64,56},{72,6... | collective-permute-start | bytes 589832 | tf_op jit(solution)/shard_map/while/body/eval_jaxpr/ppermute | solution.py:15
  222.4 10.9 %collective-permute-start.1 = (f32[3,128,128]{2,1,0:T(8,128)S(1)}, f32[3,128,128]{2,1,0:T(8,128)S(1)}, u32[]{:S(2)}, u32[]{:S(2)}) collective-permute-start(f32[3,128,128]{2,1,0:T(8,128)S(1)} %multiply_add_fusion.6), channel_id=1, source_target_pairs={{8,0},{16,8},{24,16},{32,24},{40,32},{48,40},{56,48},{64,56},{72,6... | collective-permute-start | bytes 589832 | tf_op jit(solution)/shard_map/while/body/eval_jaxpr/ppermute | solution.py:15
  233.4 11.9 %collective-permute-start.1 = (f32[3,128,128]{2,1,0:T(8,128)S(1)}, f32[3,128,128]{2,1,0:T(8,128)S(1)}, u32[]{:S(2)}, u32[]{:S(2)}) collective-permute-start(f32[3,128,128]{2,1,0:T(8,128)S(1)} %multiply_add_fusion.6), channel_id=1, source_target_pairs={{8,0},{16,8},{24,16},{32,24},{40,32},{48,40},{56,48},{64,56},{72,6... | collective-permute-start | bytes 589832 | tf_op jit(solution)/shard_map/while/body/eval_jaxpr/ppermute | solution.py:15
  245.3 11.0 %collective-permute-start.1 = (f32[3,128,128]{2,1,0:T(8,128)S(1)}, f32[3,128,128]{2,1,0:T(8,128)S(1)}, u32[]{:S(2)}, u32[]{:S(2)}) collective-permute-start(f32[3,128,128]{2,1,0:T(8,128)S(1)} %multiply_add_fusion.6), channel_id=1, source_target_pairs={{8,0},{16,8},{24,16},{32,24},{40,32},{48,40},{56,48},{64,56},{72,6... | collective-permute-start | bytes 589832 | tf_op jit(solution)/shard_map/while/body/eval_jaxpr/ppermute | solution.py:15
  256.4 10.1 %collective-permute-start.1 = (f32[3,128,128]{2,1,0:T(8,128)S(1)}, f32[3,128,128]{2,1,0:T(8,128)S(1)}, u32[]{:S(2)}, u32[]{:S(2)}) collective-permute-start(f32[3,128,128]{2,1,0:T(8,128)S(1)} %multiply_add_fusion.6), channel_id=1, source_target_pairs={{8,0},{16,8},{24,16},{32,24},{40,32},{48,40},{56,48},{64,56},{72,6... | collective-permute-start | bytes 589832 | tf_op jit(solution)/shard_map/while/body/eval_jaxpr/ppermute | solution.py:15
  325.5 10.7 %collective-permute-start.1 = (f32[3,128,128]{2,1,0:T(8,128)S(1)}, f32[3,128,128]{2,1,0:T(8,128)S(1)}, u32[]{:S(2)}, u32[]{:S(2)}) collective-permute-start(f32[3,128,128]{2,1,0:T(8,128)S(1)} %multiply_add_fusion.6), channel_id=1, source_target_pairs={{8,0},{16,8},{24,16},{32,24},{40,32},{48,40},{56,48},{64,56},{72,6... | collective-permute-start | bytes 589832 | tf_op jit(solution)/shard_map/while/body/eval_jaxpr/ppermute | solution.py:15
  336.3 12.1 %collective-permute-start.1 = (f32[3,128,128]{2,1,0:T(8,128)S(1)}, f32[3,128,128]{2,1,0:T(8,128)S(1)}, u32[]{:S(2)}, u32[]{:S(2)}) collective-permute-start(f32[3,128,128]{2,1,0:T(8,128)S(1)} %multiply_add_fusion.6), channel_id=1, source_target_pairs={{8,0},{16,8},{24,16},{32,24},{40,32},{48,40},{56,48},{64,56},{72,6... | collective-permute-start | bytes 589832 | tf_op jit(solution)/shard_map/while/body/eval_jaxpr/ppermute | solution.py:15
  369.0 9.7 %collective-permute-start = (f32[3,128,128]{2,1,0:T(8,128)S(1)}, f32[3,128,128]{2,1,0:T(8,128)S(1)}, u32[]{:S(2)}, u32[]{:S(2)}) collective-permute-start(f32[3,128,128]{2,1,0:T(8,128)S(1)} %multiply_add_fusion.5), channel_id=1, source_target_pairs={{0,8},{8,16},{16,24},{24,32},{32,40},{40,48},{48,56},{56,64},{64,7... | collective-permute-start | bytes 589832 | tf_op jit(solution)/shard_map/while/body/eval_jaxpr/ppermute | solution.py:15
  378.8 9.7 %collective-permute-start = (f32[3,128,128]{2,1,0:T(8,128)S(1)}, f32[3,128,128]{2,1,0:T(8,128)S(1)}, u32[]{:S(2)}, u32[]{:S(2)}) collective-permute-start(f32[3,128,128]{2,1,0:T(8,128)S(1)} %multiply_add_fusion.5), channel_id=1, source_target_pairs={{0,8},{8,16},{16,24},{24,32},{32,40},{40,48},{48,56},{56,64},{64,7... | collective-permute-start | bytes 589832 | tf_op jit(solution)/shard_map/while/body/eval_jaxpr/ppermute | solution.py:15
  388.6 9.7 %collective-permute-start = (f32[3,128,128]{2,1,0:T(8,128)S(1)}, f32[3,128,128]{2,1,0:T(8,128)S(1)}, u32[]{:S(2)}, u32[]{:S(2)}) collective-permute-start(f32[3,128,128]{2,1,0:T(8,128)S(1)} %multiply_add_fusion.5), channel_id=1, source_target_pairs={{0,8},{8,16},{16,24},{24,32},{32,40},{40,48},{48,56},{56,64},{64,7... | collective-permute-start | bytes 589832 | tf_op jit(solution)/shard_map/while/body/eval_jaxpr/ppermute | solution.py:15
  398.5 9.7 %collective-permute-start = (f32[3,128,128]{2,1,0:T(8,128)S(1)}, f32[3,128,128]{2,1,0:T(8,128)S(1)}, u32[]{:S(2)}, u32[]{:S(2)}) collective-permute-start(f32[3,128,128]{2,1,0:T(8,128)S(1)} %multiply_add_fusion.5), channel_id=1, source_target_pairs={{0,8},{8,16},{16,24},{24,32},{32,40},{40,48},{48,56},{56,64},{64,7... | collective-permute-start | bytes 589832 | tf_op jit(solution)/shard_map/while/body/eval_jaxpr/ppermute | solution.py:15
  408.3 9.7 %collective-permute-start = (f32[3,128,128]{2,1,0:T(8,128)S(1)}, f32[3,128,128]{2,1,0:T(8,128)S(1)}, u32[]{:S(2)}, u32[]{:S(2)}) collective-permute-start(f32[3,128,128]{2,1,0:T(8,128)S(1)} %multiply_add_fusion.5), channel_id=1, source_target_pairs={{0,8},{8,16},{16,24},{24,32},{32,40},{40,48},{48,56},{56,64},{64,7... | collective-permute-start | bytes 589832 | tf_op jit(solution)/shard_map/while/body/eval_jaxpr/ppermute | solution.py:15
  427.9 10.6 %collective-permute-start = (f32[3,128,128]{2,1,0:T(8,128)S(1)}, f32[3,128,128]{2,1,0:T(8,128)S(1)}, u32[]{:S(2)}, u32[]{:S(2)}) collective-permute-start(f32[3,128,128]{2,1,0:T(8,128)S(1)} %multiply_add_fusion.5), channel_id=1, source_target_pairs={{0,8},{8,16},{16,24},{24,32},{32,40},{40,48},{48,56},{56,64},{64,7... | collective-permute-start | bytes 589832 | tf_op jit(solution)/shard_map/while/body/eval_jaxpr/ppermute | solution.py:15
  438.7 11.8 %collective-permute-start = (f32[3,128,128]{2,1,0:T(8,128)S(1)}, f32[3,128,128]{2,1,0:T(8,128)S(1)}, u32[]{:S(2)}, u32[]{:S(2)}) collective-permute-start(f32[3,128,128]{2,1,0:T(8,128)S(1)} %multiply_add_fusion.5), channel_id=1, source_target_pairs={{0,8},{8,16},{16,24},{24,32},{32,40},{40,48},{48,56},{56,64},{64,7... | collective-permute-start | bytes 589832 | tf_op jit(solution)/shard_map/while/body/eval_jaxpr/ppermute | solution.py:15
  450.6 11.2 %collective-permute-start = (f32[3,128,128]{2,1,0:T(8,128)S(1)}, f32[3,128,128]{2,1,0:T(8,128)S(1)}, u32[]{:S(2)}, u32[]{:S(2)}) collective-permute-start(f32[3,128,128]{2,1,0:T(8,128)S(1)} %multiply_add_fusion.5), channel_id=1, source_target_pairs={{0,8},{8,16},{16,24},{24,32},{32,40},{40,48},{48,56},{56,64},{64,7... | collective-permute-start | bytes 589832 | tf_op jit(solution)/shard_map/while/body/eval_jaxpr/ppermute | solution.py:15
  461.8 10.4 %collective-permute-start = (f32[3,128,128]{2,1,0:T(8,128)S(1)}, f32[3,128,128]{2,1,0:T(8,128)S(1)}, u32[]{:S(2)}, u32[]{:S(2)}) collective-permute-start(f32[3,128,128]{2,1,0:T(8,128)S(1)} %multiply_add_fusion.5), channel_id=1, source_target_pairs={{0,8},{8,16},{16,24},{24,32},{32,40},{40,48},{48,56},{56,64},{64,7... | collective-permute-start | bytes 589832 | tf_op jit(solution)/shard_map/while/body/eval_jaxpr/ppermute | solution.py:15
  472.3 10.0 %collective-permute-start = (f32[3,128,128]{2,1,0:T(8,128)S(1)}, f32[3,128,128]{2,1,0:T(8,128)S(1)}, u32[]{:S(2)}, u32[]{:S(2)}) collective-permute-start(f32[3,128,128]{2,1,0:T(8,128)S(1)} %multiply_add_fusion.5), channel_id=1, source_target_pairs={{0,8},{8,16},{16,24},{24,32},{32,40},{40,48},{48,56},{56,64},{64,7... | collective-permute-start | bytes 589832 | tf_op jit(solution)/shard_map/while/body/eval_jaxpr/ppermute | solution.py:15
  482.4 9.7 %collective-permute-start = (f32[3,128,128]{2,1,0:T(8,128)S(1)}, f32[3,128,128]{2,1,0:T(8,128)S(1)}, u32[]{:S(2)}, u32[]{:S(2)}) collective-permute-start(f32[3,128,128]{2,1,0:T(8,128)S(1)} %multiply_add_fusion.5), channel_id=1, source_target_pairs={{0,8},{8,16},{16,24},{24,32},{32,40},{40,48},{48,56},{56,64},{64,7... | collective-permute-start | bytes 589832 | tf_op jit(solution)/shard_map/while/body/eval_jaxpr/ppermute | solution.py:15
  492.3 9.7 %collective-permute-start = (f32[3,128,128]{2,1,0:T(8,128)S(1)}, f32[3,128,128]{2,1,0:T(8,128)S(1)}, u32[]{:S(2)}, u32[]{:S(2)}) collective-permute-start(f32[3,128,128]{2,1,0:T(8,128)S(1)} %multiply_add_fusion.5), channel_id=1, source_target_pairs={{0,8},{8,16},{16,24},{24,32},{32,40},{40,48},{48,56},{56,64},{64,7... | collective-permute-start | bytes 589832 | tf_op jit(solution)/shard_map/while/body/eval_jaxpr/ppermute | solution.py:15
  502.1 9.7 %collective-permute-start = (f32[3,128,128]{2,1,0:T(8,128)S(1)}, f32[3,128,128]{2,1,0:T(8,128)S(1)}, u32[]{:S(2)}, u32[]{:S(2)}) collective-permute-start(f32[3,128,128]{2,1,0:T(8,128)S(1)} %multiply_add_fusion.5), channel_id=1, source_target_pairs={{0,8},{8,16},{16,24},{24,32},{32,40},{40,48},{48,56},{56,64},{64,7... | collective-permute-start | bytes 589832 | tf_op jit(solution)/shard_map/while/body/eval_jaxpr/ppermute | solution.py:15
  511.9 9.7 %collective-permute-start = (f32[3,128,128]{2,1,0:T(8,128)S(1)}, f32[3,128,128]{2,1,0:T(8,128)S(1)}, u32[]{:S(2)}, u32[]{:S(2)}) collective-permute-start(f32[3,128,128]{2,1,0:T(8,128)S(1)} %multiply_add_fusion.5), channel_id=1, source_target_pairs={{0,8},{8,16},{16,24},{24,32},{32,40},{40,48},{48,56},{56,64},{64,7... | collective-permute-start | bytes 589832 | tf_op jit(solution)/shard_map/while/body/eval_jaxpr/ppermute | solution.py:15
  531.5 10.4 %collective-permute-start = (f32[3,128,128]{2,1,0:T(8,128)S(1)}, f32[3,128,128]{2,1,0:T(8,128)S(1)}, u32[]{:S(2)}, u32[]{:S(2)}) collective-permute-start(f32[3,128,128]{2,1,0:T(8,128)S(1)} %multiply_add_fusion.5), channel_id=1, source_target_pairs={{0,8},{8,16},{16,24},{24,32},{32,40},{40,48},{48,56},{56,64},{64,7... | collective-permute-start | bytes 589832 | tf_op jit(solution)/shard_map/while/body/eval_jaxpr/ppermute | solution.py:15
  542.0 11.5 %collective-permute-start = (f32[3,128,128]{2,1,0:T(8,128)S(1)}, f32[3,128,128]{2,1,0:T(8,128)S(1)}, u32[]{:S(2)}, u32[]{:S(2)}) collective-permute-start(f32[3,128,128]{2,1,0:T(8,128)S(1)} %multiply_add_fusion.5), channel_id=1, source_target_pairs={{0,8},{8,16},{16,24},{24,32},{32,40},{40,48},{48,56},{56,64},{64,7... | collective-permute-start | bytes 589832 | tf_op jit(solution)/shard_map/while/body/eval_jaxpr/ppermute | solution.py:15
  553.6 11.0 %collective-permute-start = (f32[3,128,128]{2,1,0:T(8,128)S(1)}, f32[3,128,128]{2,1,0:T(8,128)S(1)}, u32[]{:S(2)}, u32[]{:S(2)}) collective-permute-start(f32[3,128,128]{2,1,0:T(8,128)S(1)} %multiply_add_fusion.5), channel_id=1, source_target_pairs={{0,8},{8,16},{16,24},{24,32},{32,40},{40,48},{48,56},{56,64},{64,7... | collective-permute-start | bytes 589832 | tf_op jit(solution)/shard_map/while/body/eval_jaxpr/ppermute | solution.py:15
  564.7 10.4 %collective-permute-start = (f32[3,128,128]{2,1,0:T(8,128)S(1)}, f32[3,128,128]{2,1,0:T(8,128)S(1)}, u32[]{:S(2)}, u32[]{:S(2)}) collective-permute-start(f32[3,128,128]{2,1,0:T(8,128)S(1)} %multiply_add_fusion.5), channel_id=1, source_target_pairs={{0,8},{8,16},{16,24},{24,32},{32,40},{40,48},{48,56},{56,64},{64,7... | collective-permute-start | bytes 589832 | tf_op jit(solution)/shard_map/while/body/eval_jaxpr/ppermute | solution.py:15
  575.1 10.0 %collective-permute-start = (f32[3,128,128]{2,1,0:T(8,128)S(1)}, f32[3,128,128]{2,1,0:T(8,128)S(1)}, u32[]{:S(2)}, u32[]{:S(2)}) collective-permute-start(f32[3,128,128]{2,1,0:T(8,128)S(1)} %multiply_add_fusion.5), channel_id=1, source_target_pairs={{0,8},{8,16},{16,24},{24,32},{32,40},{40,48},{48,56},{56,64},{64,7... | collective-permute-start | bytes 589832 | tf_op jit(solution)/shard_map/while/body/eval_jaxpr/ppermute | solution.py:15
  634.4 10.4 %collective-permute-start = (f32[3,128,128]{2,1,0:T(8,128)S(1)}, f32[3,128,128]{2,1,0:T(8,128)S(1)}, u32[]{:S(2)}, u32[]{:S(2)}) collective-permute-start(f32[3,128,128]{2,1,0:T(8,128)S(1)} %multiply_add_fusion.5), channel_id=1, source_target_pairs={{0,8},{8,16},{16,24},{24,32},{32,40},{40,48},{48,56},{56,64},{64,7... | collective-permute-start | bytes 589832 | tf_op jit(solution)/shard_map/while/body/eval_jaxpr/ppermute | solution.py:15
  644.8 11.5 %collective-permute-start = (f32[3,128,128]{2,1,0:T(8,128)S(1)}, f32[3,128,128]{2,1,0:T(8,128)S(1)}, u32[]{:S(2)}, u32[]{:S(2)}) collective-permute-start(f32[3,128,128]{2,1,0:T(8,128)S(1)} %multiply_add_fusion.5), channel_id=1, source_target_pairs={{0,8},{8,16},{16,24},{24,32},{32,40},{40,48},{48,56},{56,64},{64,7... | collective-permute-start | bytes 589832 | tf_op jit(solution)/shard_map/while/body/eval_jaxpr/ppermute | solution.py:15
  656.4 11.0 %collective-permute-start = (f32[3,128,128]{2,1,0:T(8,128)S(1)}, f32[3,128,128]{2,1,0:T(8,128)S(1)}, u32[]{:S(2)}, u32[]{:S(2)}) collective-permute-start(f32[3,128,128]{2,1,0:T(8,128)S(1)} %multiply_add_fusion.5), channel_id=1, source_target_pairs={{0,8},{8,16},{16,24},{24,32},{32,40},{40,48},{48,56},{56,64},{64,7... | collective-permute-start | bytes 589832 | tf_op jit(solution)/shard_map/while/body/eval_jaxpr/ppermute | solution.py:15
  737.1 95.7 %all-to-all-start = ((bf16[64,8,128]{2,0,1:T(8,128)(2,1)}), bf16[64,8,128]{2,0,1:T(8,128)(2,1)S(1)}, u32[]{:S(2)}, u32[]{:S(2)}) async-start(bf16[64,8,128]{2,0,1:T(8,128)(2,1)} %copy_bitcast_fusion.3), calls=%async_computation | async-start | bytes 262144 | tf_op jit(solution)/shard_map/all_to_all | solution.py:69
  822.6 50.3 %collective-permute-start.5 = (bf16[512,128]{1,0:T(8,128)(2,1)}, bf16[512,128]{1,0:T(8,128)(2,1)S(1)}, u32[]{:S(2)}, u32[]{:S(2)}) collective-permute-start(bf16[512,128]{1,0:T(8,128)(2,1)} %bitcast.18), channel_id=1, source_target_pairs={{0,8},{8,16},{16,24},{24,32},{32,40},{40,48},{48,56},{56,64},{64,7... | collective-permute-start | bytes 393224 | tf_op jit(solution)/shard_map/ppermute | solution.py:15
  827.6 44.2 %collective-permute-start.7 = (bf16[512,128]{1,0:T(8,128)(2,1)}, bf16[512,128]{1,0:T(8,128)(2,1)S(1)}, u32[]{:S(2)}, u32[]{:S(2)}) collective-permute-start(bf16[512,128]{1,0:T(8,128)(2,1)} %bitcast.18), channel_id=1, source_target_pairs={{0,24},{8,32},{16,40},{24,48},{32,56},{40,64},{48,72},{56,80},{64,... | collective-permute-start | bytes 393224 | tf_op jit(solution)/shard_map/ppermute | solution.py:15
  829.5 38.7 %collective-permute-start.6 = (bf16[512,128]{1,0:T(8,128)(2,1)}, bf16[512,128]{1,0:T(8,128)(2,1)S(1)}, u32[]{:S(2)}, u32[]{:S(2)}) collective-permute-start(bf16[512,128]{1,0:T(8,128)(2,1)} %bitcast.18), channel_id=1, source_target_pairs={{0,16},{8,24},{16,32},{24,40},{32,48},{40,56},{48,64},{56,72},{64,... | collective-permute-start | bytes 393224 | tf_op jit(solution)/shard_map/ppermute | solution.py:15
  834.8 14.5 %collective-permute-start.2 = (bf16[512,128]{1,0:T(8,128)(2,1)S(1)}, bf16[512,128]{1,0:T(8,128)(2,1)S(1)}, u32[]{:S(2)}, u32[]{:S(2)}) collective-permute-start(bf16[512,128]{1,0:T(8,128)(2,1)S(1)} %bitcast.557), channel_id=1, source_target_pairs={{0,8},{8,16},{16,24},{24,32},{32,40},{40,48},{48,56},{56,64},{64,7... | collective-permute-start | bytes 393224 | tf_op jit(solution)/shard_map/ppermute | solution.py:15
  858.8 33.8 %collective-permute-start.11 = (f32[512,1,128]{2,0,1:T(8,128)}, f32[512,1,128]{2,0,1:T(8,128)}, u32[]{:S(2)}, u32[]{:S(2)}) collective-permute-start(f32[512,1,128]{2,0,1:T(8,128)} %fusion.104), channel_id=1, source_target_pairs={{8,0},{16,8},{24,16},{32,24},{40,32},{48,40},{56,48},{64,56},{72,6... | collective-permute-start | bytes 786440 | tf_op jit(solution)/shard_map/ppermute | solution.py:15
  860.7 34.6 %collective-permute-start.12 = (f32[512,1,128]{2,0,1:T(8,128)}, f32[512,1,128]{2,0,1:T(8,128)}, u32[]{:S(2)}, u32[]{:S(2)}) collective-permute-start(f32[512,1,128]{2,0,1:T(8,128)} %fusion.107), channel_id=1, source_target_pairs={{16,0},{24,8},{32,16},{40,24},{48,32},{56,40},{64,48},{72,56},{80,... | collective-permute-start | bytes 786440 | tf_op jit(solution)/shard_map/ppermute | solution.py:15
  868.2 27.1 %collective-permute-start.13 = (f32[512,1,128]{2,0,1:T(8,128)}, f32[512,1,128]{2,0,1:T(8,128)}, u32[]{:S(2)}, u32[]{:S(2)}) collective-permute-start(f32[512,1,128]{2,0,1:T(8,128)} %fusion.110), channel_id=1, source_target_pairs={{24,0},{32,8},{40,16},{48,24},{56,32},{64,40},{72,48},{80,56},{88,... | collective-permute-start | bytes 786440 | tf_op jit(solution)/shard_map/ppermute | solution.py:15
  881.1 26.6 %collective-permute-start.8 = (f32[512,1,128]{2,0,1:T(8,128)}, f32[512,1,128]{2,0,1:T(8,128)}, u32[]{:S(2)}, u32[]{:S(2)}) collective-permute-start(f32[512,1,128]{2,0,1:T(8,128)} %fusion.140), channel_id=1, source_target_pairs={{8,0},{16,8},{24,16},{32,24},{40,32},{48,40},{56,48},{64,56},{72,6... | collective-permute-start | bytes 786440 | tf_op jit(solution)/shard_map/ppermute | solution.py:15
  883.6 24.1 %collective-permute-start.9 = (f32[512,1,128]{2,0,1:T(8,128)S(1)}, f32[512,1,128]{2,0,1:T(8,128)}, u32[]{:S(2)}, u32[]{:S(2)}) collective-permute-start(f32[512,1,128]{2,0,1:T(8,128)S(1)} %fusion.134), channel_id=1, source_target_pairs={{16,0},{24,8},{32,16},{40,24},{48,32},{56,40},{64,48},{72,56},{80,... | collective-permute-start | bytes 786440 | tf_op jit(solution)/shard_map/ppermute | solution.py:15
  892.7 15.0 %collective-permute-start.10 = (f32[512,1,128]{2,0,1:T(8,128)S(1)}, f32[512,1,128]{2,0,1:T(8,128)}, u32[]{:S(2)}, u32[]{:S(2)}) collective-permute-start(f32[512,1,128]{2,0,1:T(8,128)S(1)} %fusion.128), channel_id=1, source_target_pairs={{24,0},{32,8},{40,16},{48,24},{56,32},{64,40},{72,48},{80,56},{88,... | collective-permute-start | bytes 786440 | tf_op jit(solution)/shard_map/ppermute | solution.py:15
  899.2 13.8 %all-to-all-start.3 = ((bf16[8,64,128]{2,1,0:T(8,128)(2,1)}), bf16[8,64,128]{2,1,0:T(8,128)(2,1)S(1)}, u32[]{:S(2)}, u32[]{:S(2)}) async-start(bf16[8,64,128]{2,1,0:T(8,128)(2,1)} %bitcast.94), calls=%async_computation.3 | async-start | bytes 262144 | tf_op jit(solution)/shard_map/all_to_all | solution.py:168
  (50 other events, 2077.5 us)
where the time goes:
time: 928 us; the launch traced here: 923 us
  starting transfers between devices  414 us (45%)
  waiting for transfers between devices  367 us (40%)
  blocking collectives  59 us (6%)
  matrix products  42.3 us (5%)
  local copies, waits for them, and re-layouts  18.8 us (2%)
  other arithmetic  17.1 us (2%)
    ppermute x74, waiting for transfers between devices, from_behind(): return lax.ppermute(block, axis, route)  360 us
    ppermute x74, starting transfers between devices, from_behind(): return lax.ppermute(block, axis, route)  311 us
    all_to_all x1, starting transfers between devices, on_device(): lax.all_to_all(cache_keys, 'head', split_axis=1, concat_axis=0, tiled=True)  84.8 us
    unnamed x1, blocking collectives  59 us
  transfers between devices with their start and end apart: 78, of which 66 were waited for; matrix products, arithmetic and copies ran while one was open for 8% of the time, Pallas kernels for 0%

commit v1 on v0

--- a/solution.py
+++ b/solution.py
@@ -13,20 +13,6 @@
     devices = range(lax.axis_size(axis))
     route = [(i - distance, i) for i in devices if i - distance in devices]
     return lax.ppermute(block, axis, route)
-
-
-def prefix(part, axis, combine, identity):
-    count = lax.axis_size(axis)
-    place = lax.axis_index(axis)
-    ahead = count - 1 - place
-    gathered = lax.all_gather(part, axis)
-    state = jnp.zeros_like(part) + jnp.asarray(identity, part.dtype)
-
-    def one(step, state):
-        source = count - 1 - step
-        return combine(state, lax.dynamic_index_in_dim(gathered, source, 0, False))
-
-    return lax.fori_loop(0, ahead, one, state)
 
 
 def doc_index(offsets, positions):
@@ -40,10 +26,6 @@
     first_w = jnp.where((doc_block == before_doc)[None, :], jnp.exp(cum), 0.0)
     carried = jnp.where(final_doc == before_doc, jnp.exp(cum[:, -1]), 0.0)
     return (cum, last_w, first_w, carried)
-
-
-def add_pair(earlier, later_one):
-    return earlier + later_one
 
 
 def on_device(
@@ -185,16 +167,26 @@
         "thd,the->hde", queries_w, retained_grad, preferred_element_type=jnp.float32
     )
     zeros_state = jnp.zeros((heads_local, DH, DH), jnp.float32)
-    zeros_head = jnp.zeros((heads_local,), jnp.float32)
-
-    def relay_forward(turn, current):
-        return from_behind(carried[:, None, None] * current + own_state, "ctx", 1)
-
-    def relay_backward(turn, current):
-        return from_behind(own_grad + carried[:, None, None] * current, "ctx", -1)
-
-    state = lax.fori_loop(0, ctx_count - 1, relay_forward, zeros_state)
-    later_grad = lax.fori_loop(0, ctx_count - 1, relay_backward, zeros_state)
+
+    carried_state = jnp.concatenate(
+        [own_state.reshape(heads_local, DH * DH), jnp.broadcast_to(carried[:, None], (heads_local, DH))],
+        axis=1,
+    )
+    carried_grad = jnp.concatenate(
+        [own_grad.reshape(heads_local, DH * DH), jnp.broadcast_to(carried[:, None], (heads_local, DH))],
+        axis=1,
+    )
+    state = zeros_state
+    later_grad = zeros_state
+    forward_scale = jnp.ones((heads_local, 1, 1), jnp.float32)
+    backward_scale = jnp.ones((heads_local, 1, 1), jnp.float32)
+    for distance in range(1, DOC_DEVS + 1):
+        before = from_behind(carried_state, "ctx", distance)
+        after = from_behind(carried_grad, "ctx", -distance)
+        state = state + forward_scale * before[:, : DH * DH].reshape(heads_local, DH, DH)
+        later_grad = later_grad + backward_scale * after[:, : DH * DH].reshape(heads_local, DH, DH)
+        forward_scale = forward_scale * before[:, DH * DH :][:, :1, None]
+        backward_scale = backward_scale * after[:, DH * DH :][:, :1, None]
     state_b = state.astype(jnp.bfloat16)
     later_b = later_grad.astype(jnp.bfloat16)
     positions = jnp.arange(local_rows, dtype=jnp.int32)
@@ -230,7 +222,10 @@
     )
     residue = residue.T
     suffix = jnp.flip(jnp.cumsum(jnp.flip(residue, 1), axis=1), 1)
-    tail = prefix(suffix[:, 0], "ctx", add_pair, zeros_head)
+    totals = jnp.broadcast_to(jnp.pad(suffix[:, 0], (0, DH - heads_local))[None, :], (ctx_count, DH))
+    totals = lax.all_to_all(totals, "ctx", split_axis=0, concat_axis=0, tiled=True)
+    after_me = jnp.arange(ctx_count)[:, None] > my_rank
+    tail = jnp.sum(jnp.where(after_me, totals, 0.0), axis=0)[:heads_local]
     decay_grad = suffix + tail[:, None]
     return (
         cross_query_grad,

time: 928 us -> 212 us (0.23)
  waiting for transfers between devices: 367 us -> 9.28 us
  starting transfers between devices: 414 us -> 97.9 us
  blocking collectives: 59 us -> 0 us
  local copies, waits for them, and re-layouts: 18.8 us -> 35.8 us
    ppermute x74 -> x18, waiting for transfers between devices: 360 us -> 1.67 us  [from_behind(): return lax.ppermute(block, axis, route)]
    ppermute x74 -> x18, starting transfers between devices: 311 us -> 65 us  [from_behind(): return lax.ppermute(block, axis, route)]
    all_to_all x1, starting transfers between devices: 84.8 us -> 6.54 us  [on_device(): lax.all_to_all(cache_keys, 'head', split_axis=1, concat_axis=0, tiled=True)]
    unnamed x1 -> x0, blocking collectives: 59 us -> none
    unnamed x56 -> x66, local copies, waits for them, and re-layouts: 11.2 us -> 19.9 us
  transfers between devices with their start and end apart: 78 -> 23, of which waited for: 66 -> 3; matrix products, arithmetic and copies ran while one was open for 8% -> 41% of each run, Pallas kernels for 0% -> 0%
where the time goes in v1:
time: 212 us; the launch traced here: 210 us
  starting transfers between devices  97.9 us (46%)
  matrix products  50 us (24%)
  local copies, waits for them, and re-layouts  35.8 us (17%)
  other arithmetic  14.3 us (7%)
  waiting for transfers between devices  9.28 us (4%)
  between operations  2.73 us (1%)
    ppermute x18, starting transfers between devices, from_behind(): return lax.ppermute(block, axis, route)  65 us
    unnamed x66, local copies, waits for them, and re-layouts  19.9 us
    all_to_all x1, starting transfers between devices, on_device(): lax.all_to_all(value_flat, 'head', split_axis=0, concat_axis=1, tiled=True)  10.7 us
    dot_general x4, matrix products, on_device(): jnp.einsum('gatk,tgad->kgd', weights_b, upstream, preferred_element_type=...  9.49 us
    dot_general x4, matrix products, on_device(): jnp.einsum('tgad,kgd->gatk', upstream, grad_item[1], preferred_element_ty...  8.2 us
    dot_general x4, matrix products, on_device(): jnp.einsum('gatk,kgd->tgad', output_weights_b, item[1], preferred_element...  7.39 us
    all_to_all x1, starting transfers between devices, on_device(): lax.all_to_all(totals, 'ctx', split_axis=0, concat_axis=0, tiled=True)  6.81 us
    all_to_all x1, starting transfers between devices, on_device(): lax.all_to_all(cache_keys, 'head', split_axis=1, concat_axis=0, tiled=True)  6.54 us
  transfers between devices with their start and end apart: 23, of which 3 were waited for; matrix products, arithmetic and copies ran while one was open for 41% of the time, Pallas kernels for 0%

profile of v1, /device:TPU:103, one launch (start us, length us, event | category | flops | bytes accessed | tf_op | source)
XLA Modules:
  0.0 210.0 jit_solution(8355501827750749652)
XLA Ops:
  13.3 2.1 collective-permute-start.17
  15.4 3.6 %collective-permute-start.16 = (f32[3,16512]{1,0:T(4,128)}, f32[3,16512]{1,0:T(4,128)}, u32[]{:S(2)}, u32[]{:S(2)}) collective-permute-start(f32[3,16512]{1,0:T(4,128)} %get-tuple-element.60), channel_id=1, source_target_pairs={{16,0},{24,8},{32,16},{40,24},{48,32},{56,40},{64,48},{72,56},{80,... | collective-permute-start | bytes 594440 | tf_op jit(solution)/shard_map/ppermute | solution.py:15
  19.0 1.9 collective-permute-start.15
  21.0 5.0 %collective-permute-start.14 = (f32[3,16512]{1,0:T(4,128)}, f32[3,16512]{1,0:T(4,128)}, u32[]{:S(2)}, u32[]{:S(2)}) collective-permute-start(f32[3,16512]{1,0:T(4,128)} %get-tuple-element.61), channel_id=1, source_target_pairs={{0,24},{8,32},{16,40},{24,48},{32,56},{40,64},{48,72},{56,80},{64,... | collective-permute-start | bytes 594440 | tf_op jit(solution)/shard_map/ppermute | solution.py:15
  25.9 6.2 %collective-permute-start.13 = (f32[3,16512]{1,0:T(4,128)}, f32[3,16512]{1,0:T(4,128)}, u32[]{:S(2)}, u32[]{:S(2)}) collective-permute-start(f32[3,16512]{1,0:T(4,128)} %get-tuple-element.61), channel_id=1, source_target_pairs={{0,16},{8,24},{16,32},{24,40},{32,48},{40,56},{48,64},{56,72},{64,... | collective-permute-start | bytes 594440 | tf_op jit(solution)/shard_map/ppermute | solution.py:15
  32.8 6.5 %all-to-all-start = ((bf16[64,8,128]{2,0,1:T(8,128)(2,1)}), bf16[64,8,128]{2,0,1:T(8,128)(2,1)}, u32[]{:S(2)}, u32[]{:S(2)}) async-start(bf16[64,8,128]{2,0,1:T(8,128)(2,1)} %copy_bitcast_fusion.8), calls=%async_computation | async-start | bytes 262144 | tf_op jit(solution)/shard_map/all_to_all | solution.py:51
  39.3 2.3 %compare_and_fusion.1 = (pred[512,512]{0,1:T(8,128)(4,1)S(1)}, pred[512,512]{0,1:T(8,128)(4,1)}, pred[512,512]{0,1:T(8,128)(4,1)}, pred[512,512]{0,1:T(8,128)(4,1)}, pred[512,512]{0,1:T(8,128)(4,1)S(1)}) fusion(s32[512]{0:T(512)S(1)} %iota_add_fusion.3, s32[512]{0:T(512)S(1)} %get-tuple-element.78, s32[512]{0:T(512)S(1)} %iota_add_fusion.1, ...), kind=kLoop, calls=%fused_computation.70 | loop fusion | flops 3670016 | bytes 1327104 | tf_op jit(solution)/shard_map/and | solution.py:64
  42.8 2.4 %fusion.51 = f32[512,3,128]{0,2,1:T(8,128)} fusion(bf16[512,3,128]{0,2,1:T(8,128)(2,1)S(1)} %bitcast.600, bf16[512,3,128]{0,2,1:T(8,128)(2,1)S(1)} %bitcast.596, bf16[512,3,128]{0,2,1:T(8,128)(2,1)S(1)} %bitcast.591, f32[3,512]{1,0:T(4,128)S(1)} %bitcast.628, pred[512,512]{1,0:T(8,128)(4,1)S(1)} %copy.307), kind=kOutput, calls=%fused_computation.71 | convolution fusion | flops 407371776 | bytes 2234368 | tf_op jit(solution)/shard_map/hts,the->she/dot_general | solution.py:215
  45.2 2.2 %multiply_convert_fusion.1 = bf16[3,512,512]{2,1,0:T(8,128)(2,1)S(1)} fusion(bf16[512,3,128]{0,2,1:T(8,128)(2,1)S(1)} %bitcast.601, bf16[512,3,128]{0,2,1:T(8,128)(2,1)S(1)} %bitcast.604, f32[3,512]{1,0:T(4,128)} %bitcast.629, pred[512,512]{1,0:T(8,128)(4,1)} %copy-done.16), kind=kOutput, calls=%fused_computation.17 | convolution fusion | flops 206045184 | bytes 2627584 | tf_op jit(solution)/shard_map/thd,shd->hts/dot_general | solution.py:197
  47.4 1.5 convolution_bitcast_fusion.4
  53.4 4.8 %all-to-all-start.1 = ((bf16[64,8,128]{2,0,1:T(8,128)(2,1)}), bf16[64,8,128]{2,0,1:T(8,128)(2,1)}, u32[]{:S(2)}, u32[]{:S(2)}) async-start(bf16[64,8,128]{2,0,1:T(8,128)(2,1)} %copy_bitcast_fusion.7), calls=%async_computation.1 | async-start | bytes 262144 | tf_op jit(solution)/shard_map/all_to_all | solution.py:52
  58.2 3.9 %fusion.9 = (f32[3,512]{1,0:T(4,128)}, f32[512,512,3]{1,0,2:T(8,128)}) fusion(pred[512,512]{0,1:T(8,128)(4,1)S(1)} %get-tuple-element.56, bf16[512,128,1]{1,0,2:T(8,128)(2,1)} %bitcast.2, bf16[512,3,128]{0,2,1:T(8,128)(2,1)S(1)} %bitcast.582), kind=kOutput, calls=%fused_computation.27 | convolution fusion | flops 203684352 | bytes 3938304 | tf_op jit(solution)/shard_map/tgad,kgd->gatk/dot_general | solution.py:79
  62.0 2.8 %collective-permute-start.12 = (f32[3,16512]{1,0:T(4,128)}, f32[3,16512]{1,0:T(4,128)}, u32[]{:S(2)}, u32[]{:S(2)}) collective-permute-start(f32[3,16512]{1,0:T(4,128)} %get-tuple-element.61), channel_id=1, source_target_pairs={{0,8},{8,16},{16,24},{24,32},{32,40},{40,48},{48,56},{56,64},{64,7... | collective-permute-start | bytes 594440 | tf_op jit(solution)/shard_map/ppermute | solution.py:15
  66.5 1.7 copy.320
  68.3 1.9 collective-permute-start.3
  71.9 1.7 copy.318
  73.7 4.7 %collective-permute-start.5 = (bf16[512,128]{1,0:T(8,128)(2,1)}, bf16[512,128]{1,0:T(8,128)(2,1)}, u32[]{:S(2)}, u32[]{:S(2)}) collective-permute-start(bf16[512,128]{1,0:T(8,128)(2,1)} %bitcast.17), channel_id=1, source_target_pairs={{0,24},{8,32},{16,40},{24,48},{32,56},{40,64},{48,72},{56,80},{64,... | collective-permute-start | bytes 393224 | tf_op jit(solution)/shard_map/ppermute | solution.py:15
  80.1 1.8 copy.319
  85.3 1.4 fusion.79
  87.9 2.9 %collective-permute-start.4 = (bf16[512,128]{1,0:T(8,128)(2,1)}, bf16[512,128]{1,0:T(8,128)(2,1)S(1)}, u32[]{:S(2)}, u32[]{:S(2)}) collective-permute-start(bf16[512,128]{1,0:T(8,128)(2,1)} %bitcast.17), channel_id=1, source_target_pairs={{0,16},{8,24},{16,32},{24,40},{32,48},{40,56},{48,64},{56,72},{64,... | collective-permute-start | bytes 393224 | tf_op jit(solution)/shard_map/ppermute | solution.py:15
  91.6 4.5 %collective-permute-start.1 = (bf16[512,128]{1,0:T(8,128)(2,1)}, bf16[512,128]{1,0:T(8,128)(2,1)S(1)}, u32[]{:S(2)}, u32[]{:S(2)}) collective-permute-start(bf16[512,128]{1,0:T(8,128)(2,1)} %bitcast.1), channel_id=1, source_target_pairs={{0,16},{8,24},{16,32},{24,40},{32,48},{40,56},{48,64},{56,72},{64,... | collective-permute-start | bytes 393224 | tf_op jit(solution)/shard_map/ppermute | solution.py:15
  98.9 3.3 %collective-permute-start = (bf16[512,128]{1,0:T(8,128)(2,1)}, bf16[512,128]{1,0:T(8,128)(2,1)S(1)}, u32[]{:S(2)}, u32[]{:S(2)}) collective-permute-start(bf16[512,128]{1,0:T(8,128)(2,1)} %bitcast.1), channel_id=1, source_target_pairs={{0,8},{8,16},{16,24},{24,32},{32,40},{40,48},{48,56},{56,64},{64,7... | collective-permute-start | bytes 393224 | tf_op jit(solution)/shard_map/ppermute | solution.py:15
  106.1 6.8 %all-to-all-start.4 = ((f32[32,1,128]{2,1,0:T(1,128)}), f32[32,1,128]{2,1,0:T(1,128)S(1)}, u32[]{:S(2)}, u32[]{:S(2)}) async-start(f32[32,1,128]{2,1,0:T(1,128)} %broadcast_in_dim.217), calls=%async_computation.4 | async-start | bytes 32768 | tf_op jit(solution)/shard_map/all_to_all | solution.py:226
  112.9 1.4 fusion.85
  118.2 4.8 %collective-permute-start.2 = (bf16[512,128]{1,0:T(8,128)(2,1)}, bf16[512,128]{1,0:T(8,128)(2,1)S(1)}, u32[]{:S(2)}, u32[]{:S(2)}) collective-permute-start(bf16[512,128]{1,0:T(8,128)(2,1)} %bitcast.1), channel_id=1, source_target_pairs={{0,24},{8,32},{16,40},{24,48},{32,56},{40,64},{48,72},{56,80},{64,... | collective-permute-start | bytes 393224 | tf_op jit(solution)/shard_map/ppermute | solution.py:15
  123.7 1.6 collective-permute-done.2
  130.6 1.8 fusion.110
  132.5 1.8 fusion.107
  134.3 1.8 fusion.104
  136.1 2.2 %collective-permute-start.9 = (f32[512,1,128]{2,0,1:T(8,128)}, f32[512,1,128]{2,0,1:T(8,128)}, u32[]{:S(2)}, u32[]{:S(2)}) collective-permute-start(f32[512,1,128]{2,0,1:T(8,128)} %fusion.104), channel_id=1, source_target_pairs={{8,0},{16,8},{24,16},{32,24},{40,32},{48,40},{56,48},{64,56},{72,6... | collective-permute-start | bytes 786440 | tf_op jit(solution)/shard_map/ppermute | solution.py:15
  138.3 4.1 %collective-permute-start.10 = (f32[512,1,128]{2,0,1:T(8,128)}, f32[512,1,128]{2,0,1:T(8,128)}, u32[]{:S(2)}, u32[]{:S(2)}) collective-permute-start(f32[512,1,128]{2,0,1:T(8,128)} %fusion.107), channel_id=1, source_target_pairs={{16,0},{24,8},{32,16},{40,24},{48,32},{56,40},{64,48},{72,56},{80,... | collective-permute-start | bytes 786440 | tf_op jit(solution)/shard_map/ppermute | solution.py:15
  142.4 2.0 fusion.44
  144.5 3.9 %collective-permute-start.11 = (f32[512,1,128]{2,0,1:T(8,128)}, f32[512,1,128]{2,0,1:T(8,128)}, u32[]{:S(2)}, u32[]{:S(2)}) collective-permute-start(f32[512,1,128]{2,0,1:T(8,128)} %fusion.110), channel_id=1, source_target_pairs={{24,0},{32,8},{40,16},{48,24},{56,32},{64,40},{72,48},{80,56},{88,... | collective-permute-start | bytes 786440 | tf_op jit(solution)/shard_map/ppermute | solution.py:15
  149.5 2.1 fusion.32
  151.6 2.2 %fusion.89 = f32[512,3]{0,1:T(4,128)S(1)} fusion(f32[512,1,3,128]{0,3,2,1:T(8,128)S(1)} %bitcast.615, f32[3,512,128]{1,2,0:T(8,128)S(1)} %fusion.32, f32[3,512,128]{1,2,0:T(8,128)S(1)} %fusion.36, f32[3,512,128]{1,2,0:T(8,128)S(1)} %fusion.44, bf16[512,128]{1,0:T(8,128)(2,1)} %collective-permute-done.3, f32[3,512]{1,0:T(4,128)S(1)} %multiply_add_fusion, ...), kind=kOutput, calls=%fused_computation.94 | convolution fusion | flops 207026688 | bytes 6703104 | tf_op jit(solution)/shard_map/gatk,kgd->tgad/dot_general | solution.py:106
  153.8 2.3 %fusion.7 = bf16[1,3,512,512]{2,3,1,0:T(8,128)(2,1)S(1)} fusion(bf16[512,128,1]{1,0,2:T(8,128)(2,1)} %bitcast.18, bf16[512,3,128]{0,2,1:T(8,128)(2,1)S(1)} %bitcast.620, f32[3,512]{1,0:T(4,128)S(1)} %bitcast.634, f32[3,512]{1,0:T(4,128)S(1)} %multiply_add_fusion, f32[3,512]{1,0:T(4,128)S(1)} %get-tuple-element.46, f32[512,512,3]{1,0,2:T(8,128)S(1)} %copy-done.1, ...), kind=kOutput, calls=%fused_computation.11 | convolution fusion | flops 207618048 | bytes 5523456 | tf_op jit(solution)/shard_map/tgad,kgd->gatk/dot_general | solution.py:121
  156.1 1.4 fusion.3
  158.7 2.3 %fusion.5 = bf16[1,3,512,512]{2,3,1,0:T(8,128)(2,1)S(1)} fusion(bf16[512,3,128]{0,2,1:T(8,128)(2,1)S(1)} %bitcast.622, f32[3,512]{1,0:T(4,128)S(1)} %bitcast.636, f32[3,512]{1,0:T(4,128)S(1)} %multiply_add_fusion, f32[3,512]{1,0:T(4,128)S(1)} %get-tuple-element.46, f32[512,512,3]{1,0,2:T(8,128)S(1)} %get-tuple-element.70, ...), kind=kOutput, calls=%fused_computation.8 | convolution fusion | flops 207618048 | bytes 5523456 | tf_op jit(solution)/shard_map/tgad,kgd->gatk/dot_general | solution.py:121
  162.3 2.5 %collective-permute-start.6 = (f32[512,1,128]{2,0,1:T(8,128)}, f32[512,1,128]{2,0,1:T(8,128)}, u32[]{:S(2)}, u32[]{:S(2)}) collective-permute-start(f32[512,1,128]{2,0,1:T(8,128)} %fusion.140), channel_id=1, source_target_pairs={{8,0},{16,8},{24,16},{32,24},{40,32},{48,40},{56,48},{64,56},{72,6... | collective-permute-start | bytes 786440 | tf_op jit(solution)/shard_map/ppermute | solution.py:15
  164.8 3.7 %collective-permute-start.7 = (f32[512,1,128]{2,0,1:T(8,128)}, f32[512,1,128]{2,0,1:T(8,128)}, u32[]{:S(2)}, u32[]{:S(2)}) collective-permute-start(f32[512,1,128]{2,0,1:T(8,128)} %fusion.134), channel_id=1, source_target_pairs={{16,0},{24,8},{32,16},{40,24},{48,32},{56,40},{64,48},{72,56},{80,... | collective-permute-start | bytes 786440 | tf_op jit(solution)/shard_map/ppermute | solution.py:15
  169.8 2.3 %fusion.1 = bf16[1,3,512,512]{2,3,1,0:T(8,128)(2,1)S(1)} fusion(bf16[512,3,128]{0,2,1:T(8,128)(2,1)S(1)} %bitcast.623, f32[3,512]{1,0:T(4,128)S(1)} %bitcast.637, f32[3,512]{1,0:T(4,128)S(1)} %multiply_add_fusion, f32[3,512]{1,0:T(4,128)S(1)} %get-tuple-element.46, f32[512,512,3]{1,0,2:T(8,128)S(1)} %get-tuple-element.66, ...), kind=kOutput, calls=%fused_computation.2 | convolution fusion | flops 207618048 | bytes 5523456 | tf_op jit(solution)/shard_map/tgad,kgd->gatk/dot_general | solution.py:121
  175.0 5.0 %collective-permute-start.8 = (f32[512,1,128]{2,0,1:T(8,128)S(1)}, f32[512,1,128]{2,0,1:T(8,128)S(1)}, u32[]{:S(2)}, u32[]{:S(2)}) collective-permute-start(f32[512,1,128]{2,0,1:T(8,128)S(1)} %fusion.128), channel_id=1, source_target_pairs={{24,0},{32,8},{40,16},{48,24},{56,32},{64,40},{72,48},{80,56},{88,... | collective-permute-start | bytes 786440 | tf_op jit(solution)/shard_map/ppermute | solution.py:15
  180.0 4.0 %fusion.161 = bf16[512,1,128]{2,0,1:T(8,128)(2,1)} fusion(f32[512,1,128]{2,0,1:T(8,128)} %collective-permute-done.11, f32[512,1,128]{2,0,1:T(8,128)} %collective-permute-done.10, f32[512,1,128]{2,0,1:T(8,128)} %collective-permute-done.9, bf16[512,3,128]{0,2,1:T(8,128)(2,1)} %bitcast.616, f32[3,512]{1,0:T(4,128)S(1)} %multiply_add_fusion, ...), kind=kOutput, calls=%fused_computation.118 | convolution fusion | flops 206307328 | bytes 4730880 | tf_op jit(solution)/shard_map/gatk,tgad->kgd/dot_general | solution.py:132
  184.0 10.7 %all-to-all-start.3 = ((bf16[8,64,128]{2,1,0:T(8,128)(2,1)}), bf16[8,64,128]{2,1,0:T(8,128)(2,1)S(1)}, u32[]{:S(2)}, u32[]{:S(2)}) async-start(bf16[8,64,128]{2,1,0:T(8,128)(2,1)} %bitcast.93), calls=%async_computation.3 | async-start | bytes 262144 | tf_op jit(solution)/shard_map/all_to_all | solution.py:150
  194.7 2.3 %fusion.158 = bf16[512,1,128]{2,0,1:T(8,128)(2,1)} fusion(f32[512,1,128]{2,0,1:T(8,128)S(1)} %collective-permute-done.8, f32[512,1,128]{2,0,1:T(8,128)} %collective-permute-done.7, f32[512,1,128]{2,0,1:T(8,128)} %collective-permute-done.6, bf16[512,3,128]{0,2,1:T(8,128)(2,1)S(1)} %bitcast.589, bf16[1,3,512,512]{2,3,1,0:T(8,128)(2,1)S(1)} %copy-done.3), kind=kOutput, calls=%fused_computation.117 | convolution fusion | flops 201654272 | bytes 2883584 | tf_op jit(solution)/shard_map/gatk,tgad->kgd/dot_general | solution.py:129
  196.9 3.0 %all-to-all-done.3 = bf16[8,64,128]{2,1,0:T(8,128)(2,1)S(1)} async-done(((bf16[8,64,128]{2,1,0:T(8,128)(2,1)}), bf16[8,64,128]{2,1,0:T(8,128)(2,1)S(1)}, u32[]{:S(2)}, u32[]{:S(2)}) %all-to-all-start.3) | async-done | bytes 131104 | tf_op jit(solution)/shard_map/all_to_all | solution.py:150
  199.9 4.1 %all-to-all-start.2 = ((bf16[8,64,128]{2,1,0:T(8,128)(2,1)}), bf16[8,64,128]{2,1,0:T(8,128)(2,1)S(1)}, u32[]{:S(2)}, u32[]{:S(2)}) async-start(bf16[8,64,128]{2,1,0:T(8,128)(2,1)} %bitcast.75), calls=%async_computation.2 | async-start | bytes 262144 | tf_op jit(solution)/shard_map/all_to_all | solution.py:149
  204.7 4.6 %all-to-all-done.2 = bf16[8,64,128]{2,1,0:T(8,128)(2,1)S(1)} async-done(((bf16[8,64,128]{2,1,0:T(8,128)(2,1)}), bf16[8,64,128]{2,1,0:T(8,128)(2,1)S(1)}, u32[]{:S(2)}, u32[]{:S(2)}) %all-to-all-start.2) | async-done | bytes 131104 | tf_op jit(solution)/shard_map/all_to_all | solution.py:149
  (154 shorter events, 53.6 us)
Async XLA Ops:
  0.6 31.5 %copy-start = (bf16[64,1024]{1,0:T(8,128)(2,1)S(1)}, bf16[64,1024]{1,0:T(8,128)(2,1)}, u32[]{:S(2)}) copy-start(bf16[64,1024]{1,0:T(8,128)(2,1)} %param.12) | copy-start | bytes 393220
  0.6 11.1 %copy-start.14 = (bf16[512,384]{1,0:T(8,128)(2,1)S(1)}, bf16[512,384]{1,0:T(8,128)(2,1)}, u32[]{:S(2)}) copy-start(bf16[512,384]{1,0:T(8,128)(2,1)} %param.17) | copy-start | bytes 1179652
  7.5 34.6 %copy-start.19 = (f32[1,3,4,128]{3,1,2,0:T(4,128)}, f32[1,3,4,128]{3,1,2,0:T(4,128)S(1)}, u32[]{:S(2)}) copy-start(f32[1,3,4,128]{3,1,2,0:T(4,128)S(1)} %copy.428) | copy-start | bytes 18436
  11.2 34.0 %copy-start.4 = (bf16[512,384]{0,1:T(8,128)(2,1)}, bf16[512,384]{0,1:T(8,128)(2,1)S(1)}, u32[]{:S(2)}) copy-start(bf16[512,384]{0,1:T(8,128)(2,1)S(1)} %copy.309) | copy-start | bytes 1179652
  13.3 48.7 %collective-permute-start.17 = (f32[3,16512]{1,0:T(4,128)}, f32[3,16512]{1,0:T(4,128)}, u32[]{:S(2)}, u32[]{:S(2)}) collective-permute-start(f32[3,16512]{1,0:T(4,128)} %get-tuple-element.60), channel_id=1, source_target_pairs={{24,0},{32,8},{40,16},{48,24},{56,32},{64,40},{72,48},{80,56},{88,... | collective-permute-start | bytes 594440 | tf_op jit(solution)/shard_map/ppermute | solution.py:15
  15.4 52.9 %collective-permute-start.16 = (f32[3,16512]{1,0:T(4,128)}, f32[3,16512]{1,0:T(4,128)}, u32[]{:S(2)}, u32[]{:S(2)}) collective-permute-start(f32[3,16512]{1,0:T(4,128)} %get-tuple-element.60), channel_id=1, source_target_pairs={{16,0},{24,8},{32,16},{40,24},{48,32},{56,40},{64,48},{72,56},{80,... | collective-permute-start | bytes 594440 | tf_op jit(solution)/shard_map/ppermute | solution.py:15
  19.0 54.7 %collective-permute-start.15 = (f32[3,16512]{1,0:T(4,128)}, f32[3,16512]{1,0:T(4,128)}, u32[]{:S(2)}, u32[]{:S(2)}) collective-permute-start(f32[3,16512]{1,0:T(4,128)} %get-tuple-element.60), channel_id=1, source_target_pairs={{8,0},{16,8},{24,16},{32,24},{40,32},{48,40},{56,48},{64,56},{72,6... | collective-permute-start | bytes 594440 | tf_op jit(solution)/shard_map/ppermute | solution.py:15
  21.0 77.9 %collective-permute-start.14 = (f32[3,16512]{1,0:T(4,128)}, f32[3,16512]{1,0:T(4,128)}, u32[]{:S(2)}, u32[]{:S(2)}) collective-permute-start(f32[3,16512]{1,0:T(4,128)} %get-tuple-element.61), channel_id=1, source_target_pairs={{0,24},{8,32},{16,40},{24,48},{32,56},{40,64},{48,72},{56,80},{64,... | collective-permute-start | bytes 594440 | tf_op jit(solution)/shard_map/ppermute | solution.py:15
  25.9 61.9 %collective-permute-start.13 = (f32[3,16512]{1,0:T(4,128)}, f32[3,16512]{1,0:T(4,128)}, u32[]{:S(2)}, u32[]{:S(2)}) collective-permute-start(f32[3,16512]{1,0:T(4,128)} %get-tuple-element.61), channel_id=1, source_target_pairs={{0,16},{8,24},{16,32},{24,40},{32,48},{40,56},{48,64},{56,72},{64,... | collective-permute-start | bytes 594440 | tf_op jit(solution)/shard_map/ppermute | solution.py:15
  32.8 20.6 %all-to-all-start = ((bf16[64,8,128]{2,0,1:T(8,128)(2,1)}), bf16[64,8,128]{2,0,1:T(8,128)(2,1)}, u32[]{:S(2)}, u32[]{:S(2)}) async-start(bf16[64,8,128]{2,0,1:T(8,128)(2,1)} %copy_bitcast_fusion.8), calls=%async_computation | async-start | bytes 262144 | tf_op jit(solution)/shard_map/all_to_all | solution.py:51
  42.1 0.7 copy-start.16
  45.2 3.8 %copy-start.17 = (bf16[64,1024]{1,0:T(8,128)(2,1)S(1)}, bf16[64,1024]{1,0:T(8,128)(2,1)}, u32[]{:S(2)}) copy-start(bf16[64,1024]{1,0:T(8,128)(2,1)} %param.13) | copy-start | bytes 393220
  47.4 2.2 %copy-start.10 = (bf16[512,384]{1,0:T(8,128)(2,1)S(1)}, bf16[512,384]{1,0:T(8,128)(2,1)}, u32[]{:S(2)}) copy-start(bf16[512,384]{1,0:T(8,128)(2,1)} %param.11) | copy-start | bytes 1179652
  53.4 14.9 %all-to-all-start.1 = ((bf16[64,8,128]{2,0,1:T(8,128)(2,1)}), bf16[64,8,128]{2,0,1:T(8,128)(2,1)}, u32[]{:S(2)}, u32[]{:S(2)}) async-start(bf16[64,8,128]{2,0,1:T(8,128)(2,1)} %copy_bitcast_fusion.7), calls=%async_computation.1 | async-start | bytes 262144 | tf_op jit(solution)/shard_map/all_to_all | solution.py:52
  62.0 29.5 %collective-permute-start.12 = (f32[3,16512]{1,0:T(4,128)}, f32[3,16512]{1,0:T(4,128)}, u32[]{:S(2)}, u32[]{:S(2)}) collective-permute-start(f32[3,16512]{1,0:T(4,128)} %get-tuple-element.61), channel_id=1, source_target_pairs={{0,8},{8,16},{16,24},{24,32},{32,40},{40,48},{48,56},{56,64},{64,7... | collective-permute-start | bytes 594440 | tf_op jit(solution)/shard_map/ppermute | solution.py:15
  68.3 83.3 %collective-permute-start.3 = (bf16[512,128]{1,0:T(8,128)(2,1)}, bf16[512,128]{1,0:T(8,128)(2,1)}, u32[]{:S(2)}, u32[]{:S(2)}) collective-permute-start(bf16[512,128]{1,0:T(8,128)(2,1)} %bitcast.17), channel_id=1, source_target_pairs={{0,8},{8,16},{16,24},{24,32},{32,40},{40,48},{48,56},{56,64},{64,7... | collective-permute-start | bytes 393224 | tf_op jit(solution)/shard_map/ppermute | solution.py:15
  73.7 75.8 %collective-permute-start.5 = (bf16[512,128]{1,0:T(8,128)(2,1)}, bf16[512,128]{1,0:T(8,128)(2,1)}, u32[]{:S(2)}, u32[]{:S(2)}) collective-permute-start(bf16[512,128]{1,0:T(8,128)(2,1)} %bitcast.17), channel_id=1, source_target_pairs={{0,24},{8,32},{16,40},{24,48},{32,56},{40,64},{48,72},{56,80},{64,... | collective-permute-start | bytes 393224 | tf_op jit(solution)/shard_map/ppermute | solution.py:15
  84.7 0.6 copy-start.11
  85.3 17.8 %copy-start.5 = (f32[512,3,128]{0,2,1:T(8,128)S(1)}, f32[512,3,128]{0,2,1:T(8,128)}, u32[]{:S(2)}) copy-start(f32[512,3,128]{0,2,1:T(8,128)} %convolution_bitcast_fusion.4) | copy-start | bytes 2359300
  87.9 25.1 %copy-start.12 = (bf16[3,128,128]{1,2,0:T(8,128)(2,1)S(1)}, bf16[3,128,128]{1,2,0:T(8,128)(2,1)}, u32[]{:S(2)}) copy-start(bf16[3,128,128]{1,2,0:T(8,128)(2,1)} %copy-done.11) | copy-start | bytes 294916
  87.9 56.6 %collective-permute-start.4 = (bf16[512,128]{1,0:T(8,128)(2,1)}, bf16[512,128]{1,0:T(8,128)(2,1)S(1)}, u32[]{:S(2)}, u32[]{:S(2)}) collective-permute-start(bf16[512,128]{1,0:T(8,128)(2,1)} %bitcast.17), channel_id=1, source_target_pairs={{0,16},{8,24},{16,32},{24,40},{32,48},{40,56},{48,64},{56,72},{64,... | collective-permute-start | bytes 393224 | tf_op jit(solution)/shard_map/ppermute | solution.py:15
  91.6 26.6 %collective-permute-start.1 = (bf16[512,128]{1,0:T(8,128)(2,1)}, bf16[512,128]{1,0:T(8,128)(2,1)S(1)}, u32[]{:S(2)}, u32[]{:S(2)}) collective-permute-start(bf16[512,128]{1,0:T(8,128)(2,1)} %bitcast.1), channel_id=1, source_target_pairs={{0,16},{8,24},{16,32},{24,40},{32,48},{40,56},{48,64},{56,72},{64,... | collective-permute-start | bytes 393224 | tf_op jit(solution)/shard_map/ppermute | solution.py:15
  98.9 17.7 %copy-start.9 = (bf16[512,3,128]{0,2,1:T(8,128)(2,1)S(1)}, bf16[512,3,128]{0,2,1:T(8,128)(2,1)}, u32[]{:S(2)}) copy-start(bf16[512,3,128]{0,2,1:T(8,128)(2,1)} %get-tuple-element.50) | copy-start | bytes 1179652
  98.9 27.2 %collective-permute-start = (bf16[512,128]{1,0:T(8,128)(2,1)}, bf16[512,128]{1,0:T(8,128)(2,1)S(1)}, u32[]{:S(2)}, u32[]{:S(2)}) collective-permute-start(bf16[512,128]{1,0:T(8,128)(2,1)} %bitcast.1), channel_id=1, source_target_pairs={{0,8},{8,16},{16,24},{24,32},{32,40},{40,48},{48,56},{56,64},{64,7... | collective-permute-start | bytes 393224 | tf_op jit(solution)/shard_map/ppermute | solution.py:15
  103.2 14.3 %copy-start.20 = (pred[32]{0:T(512)(128)(4,1)S(1)}, pred[32]{0:T(512)(128)(4,1)}, u32[]{:S(2)}) copy-start(pred[32]{0:T(512)(128)(4,1)} %iota_compare_fusion.1) | copy-start | bytes 100
  103.2 19.8 %copy-start.8 = (pred[512,512]{0,1:T(8,128)(4,1)S(1)}, pred[512,512]{0,1:T(8,128)(4,1)}, u32[]{:S(2)}) copy-start(pred[512,512]{0,1:T(8,128)(4,1)} %get-tuple-element.57) | copy-start | bytes 786436
  106.1 11.4 %all-to-all-start.4 = ((f32[32,1,128]{2,1,0:T(1,128)}), f32[32,1,128]{2,1,0:T(1,128)S(1)}, u32[]{:S(2)}, u32[]{:S(2)}) async-start(f32[32,1,128]{2,1,0:T(1,128)} %broadcast_in_dim.217), calls=%async_computation.4 | async-start | bytes 32768 | tf_op jit(solution)/shard_map/all_to_all | solution.py:226
  114.7 10.7 %copy-start.6 = (pred[512,512]{0,1:T(8,128)(4,1)S(1)}, pred[512,512]{0,1:T(8,128)(4,1)}, u32[]{:S(2)}) copy-start(pred[512,512]{0,1:T(8,128)(4,1)} %get-tuple-element.58) | copy-start | bytes 786436
  118.2 7.1 %collective-permute-start.2 = (bf16[512,128]{1,0:T(8,128)(2,1)}, bf16[512,128]{1,0:T(8,128)(2,1)S(1)}, u32[]{:S(2)}, u32[]{:S(2)}) collective-permute-start(bf16[512,128]{1,0:T(8,128)(2,1)} %bitcast.1), channel_id=1, source_target_pairs={{0,24},{8,32},{16,40},{24,48},{32,56},{40,64},{48,72},{56,80},{64,... | collective-permute-start | bytes 393224 | tf_op jit(solution)/shard_map/ppermute | solution.py:15
  123.0 3.1 %copy-start.7 = (pred[512,512]{0,1:T(8,128)(4,1)S(1)}, pred[512,512]{0,1:T(8,128)(4,1)}, u32[]{:S(2)}) copy-start(pred[512,512]{0,1:T(8,128)(4,1)} %get-tuple-element.59) | copy-start | bytes 786436
  125.3 1.4 copy-start.18
  125.4 1.9 copy-start.1
  128.9 1.7 copy-start.15
  136.1 38.9 %collective-permute-start.9 = (f32[512,1,128]{2,0,1:T(8,128)}, f32[512,1,128]{2,0,1:T(8,128)}, u32[]{:S(2)}, u32[]{:S(2)}) collective-permute-start(f32[512,1,128]{2,0,1:T(8,128)} %fusion.104), channel_id=1, source_target_pairs={{8,0},{16,8},{24,16},{32,24},{40,32},{48,40},{56,48},{64,56},{72,6... | collective-permute-start | bytes 786440 | tf_op jit(solution)/shard_map/ppermute | solution.py:15
  138.3 41.7 %collective-permute-start.10 = (f32[512,1,128]{2,0,1:T(8,128)}, f32[512,1,128]{2,0,1:T(8,128)}, u32[]{:S(2)}, u32[]{:S(2)}) collective-permute-start(f32[512,1,128]{2,0,1:T(8,128)} %fusion.107), channel_id=1, source_target_pairs={{16,0},{24,8},{32,16},{40,24},{48,32},{56,40},{64,48},{72,56},{80,... | collective-permute-start | bytes 786440 | tf_op jit(solution)/shard_map/ppermute | solution.py:15
  144.5 35.5 %collective-permute-start.11 = (f32[512,1,128]{2,0,1:T(8,128)}, f32[512,1,128]{2,0,1:T(8,128)}, u32[]{:S(2)}, u32[]{:S(2)}) collective-permute-start(f32[512,1,128]{2,0,1:T(8,128)} %fusion.110), channel_id=1, source_target_pairs={{24,0},{32,8},{40,16},{48,24},{56,32},{64,40},{72,48},{80,56},{88,... | collective-permute-start | bytes 786440 | tf_op jit(solution)/shard_map/ppermute | solution.py:15
  149.5 2.1 %copy-start.13 = (f32[512,384]{0,1:T(8,128)S(1)}, f32[512,384]{0,1:T(8,128)}, u32[]{:S(2)}) copy-start(f32[512,384]{0,1:T(8,128)} %copy.277) | copy-start | bytes 2359300
  156.1 12.4 %copy-start.2 = (bf16[1,3,512,512]{2,3,1,0:T(8,128)(2,1)}, bf16[1,3,512,512]{2,3,1,0:T(8,128)(2,1)S(1)}, u32[]{:S(2)}) copy-start(bf16[1,3,512,512]{2,3,1,0:T(8,128)(2,1)S(1)} %fusion.7) | copy-start | bytes 4718596
  162.3 32.4 %collective-permute-start.6 = (f32[512,1,128]{2,0,1:T(8,128)}, f32[512,1,128]{2,0,1:T(8,128)}, u32[]{:S(2)}, u32[]{:S(2)}) collective-permute-start(f32[512,1,128]{2,0,1:T(8,128)} %fusion.140), channel_id=1, source_target_pairs={{8,0},{16,8},{24,16},{32,24},{40,32},{48,40},{56,48},{64,56},{72,6... | collective-permute-start | bytes 786440 | tf_op jit(solution)/shard_map/ppermute | solution.py:15
  164.8 29.9 %collective-permute-start.7 = (f32[512,1,128]{2,0,1:T(8,128)}, f32[512,1,128]{2,0,1:T(8,128)}, u32[]{:S(2)}, u32[]{:S(2)}) collective-permute-start(f32[512,1,128]{2,0,1:T(8,128)} %fusion.134), channel_id=1, source_target_pairs={{16,0},{24,8},{32,16},{40,24},{48,32},{56,40},{64,48},{72,56},{80,... | collective-permute-start | bytes 786440 | tf_op jit(solution)/shard_map/ppermute | solution.py:15
  175.0 19.7 %copy-start.3 = (bf16[1,3,512,512]{2,3,1,0:T(8,128)(2,1)S(1)}, bf16[1,3,512,512]{2,3,1,0:T(8,128)(2,1)}, u32[]{:S(2)}) copy-start(bf16[1,3,512,512]{2,3,1,0:T(8,128)(2,1)} %copy-done.2) | copy-start | bytes 4718596
  175.0 19.7 %collective-permute-start.8 = (f32[512,1,128]{2,0,1:T(8,128)S(1)}, f32[512,1,128]{2,0,1:T(8,128)S(1)}, u32[]{:S(2)}, u32[]{:S(2)}) collective-permute-start(f32[512,1,128]{2,0,1:T(8,128)S(1)} %fusion.128), channel_id=1, source_target_pairs={{24,0},{32,8},{40,16},{48,24},{56,32},{64,40},{72,48},{80,56},{88,... | collective-permute-start | bytes 786440 | tf_op jit(solution)/shard_map/ppermute | solution.py:15
  184.0 16.0 %all-to-all-start.3 = ((bf16[8,64,128]{2,1,0:T(8,128)(2,1)}), bf16[8,64,128]{2,1,0:T(8,128)(2,1)S(1)}, u32[]{:S(2)}, u32[]{:S(2)}) async-start(bf16[8,64,128]{2,1,0:T(8,128)(2,1)} %bitcast.93), calls=%async_computation.3 | async-start | bytes 262144 | tf_op jit(solution)/shard_map/all_to_all | solution.py:150
  199.9 9.4 %all-to-all-start.2 = ((bf16[8,64,128]{2,1,0:T(8,128)(2,1)}), bf16[8,64,128]{2,1,0:T(8,128)(2,1)S(1)}, u32[]{:S(2)}, u32[]{:S(2)}) async-start(bf16[8,64,128]{2,1,0:T(8,128)(2,1)} %bitcast.75), calls=%async_computation.2 | async-start | bytes 262144 | tf_op jit(solution)/shard_map/all_to_all | solution.py:149

commit v2 on v0

v2 whole, which is shorter than its diff:
```python
import jax
import jax.numpy as jnp
from jax import lax
from jax.experimental import pallas as pl
from jax.experimental.pallas import tpu as pltpu
from jax.sharding import PartitionSpec as P

ATTENDER_NUMBER = 24
KV_HEADS = 8
DH = 128
PER_GROUP = ATTENDER_NUMBER // KV_HEADS
ROWS = 512
TILE = 256
TILES = ROWS // TILE
X_RING = 4
SCALING = DH ** (-0.5)
EXPONENT_SCALE = SCALING * 1.4426950408889634
MESH = pl.DeviceIdType.MESH
BF16 = jnp.bfloat16
F32 = jnp.float32
STATE_ROWS = PER_GROUP * DH + 8


def matmul(a, b):
    return lax.dot_general(a, b, (((1,), (0,)), ((), ())), preferred_element_type=F32)


def matmul_nt(a, b):
    return lax.dot_general(a, b, (((1,), (1,)), ((), ())), preferred_element_type=F32)


def matmul_tn(a, b):
    return lax.dot_general(a, b, (((0,), (0,)), ((), ())), preferred_element_type=F32)


def exact_pieces(x):
    high = x.astype(BF16)
    rest = x - high.astype(F32)
    middle = rest.astype(BF16)
    low = (rest - middle.astype(F32)).astype(BF16)
    return jnp.concatenate([high, middle, low], axis=0)


def triangle_sum(x, triangle):
    parts = matmul(exact_pieces(x), triangle)
    return parts[0:16] + parts[16:32] + parts[32:48]


def body(
    n_ctx, n_head,
    cq, cg, ck, cv, rq, rk, rv, rg, ld, offs,
    gq, gk, gv, oq, ok, ov, dg,
    kvs, kvb, own_f, own_b, got_f, got_b, part, half, back, home, final, landed, tot_x, tot_z,
    qs, os, kt, score, dprob, prob_t, dscore_t,
    start_row, cum_row, cum_col, last_w, first_w, qf, kf, vf, pad16,
    head_s, head_r, kv_s, kv_r, st_s, st_r, gr_s, gr_r, fin_s, fin_r, tx_s, tx_r, tz_s, tz_r,
):
    c = lax.axis_index("ctx")
    g = lax.axis_index("head")
    z_ring = n_ctx // X_RING
    slot_rows = ROWS // n_head

    def ctx_at(offset):
        return lax.rem(c + (offset + n_ctx), n_ctx)

    def head_at(offset):
        return lax.rem(g + offset, n_head)

    x = lax.rem(c, X_RING)
    z = c // X_RING

    def x_peer(offset):
        return z * X_RING + lax.rem(x + offset, X_RING)

    def z_peer(offset):
        return lax.rem(z + offset, z_ring) * X_RING + x

    def send(src, dst, send_sem, recv_sem, device):
        return pltpu.make_async_remote_copy(
            src_ref=src, dst_ref=dst, send_sem=send_sem, recv_sem=recv_sem,
            device_id=device, device_id_type=MESH,
        )

    partners = [(c, head_at(k)) for k in range(1, n_head)]
    partners += [(ctx_at(k), g) for k in (1, -1, 3, -3)]
    partners += [(x_peer(k), g) for k in range(1, X_RING)]
    partners += [(z_peer(k), g) for k in range(1, z_ring)]
    barrier = pltpu.get_barrier_semaphore()
    for device in partners:
        pl.semaphore_signal(barrier, inc=1, device_id=device, device_id_type=MESH)

    kvs[0] = ck[...]
    kvs[1] = cv[...]
    base = (c * ROWS).astype(F32)
    offsets = offs[...].astype(F32)
    pos_col = lax.broadcasted_iota(jnp.int32, (ROWS, 1), 0).astype(F32)
    begun = jnp.where(offsets <= pos_col + base, offsets, 0.0)
    start_col = jnp.max(begun, axis=1, keepdims=True) - base
    start_row[...] = jnp.broadcast_to(start_col, (ROWS, DH)).T[0:8]
    start_last = start_col[ROWS - 1 : ROWS, :]
    row_at = lax.broadcasted_iota(jnp.int32, (ROWS, ROWS), 0)
    col_at = lax.broadcasted_iota(jnp.int32, (ROWS, ROWS), 1)

    pl.semaphore_wait(barrier, len(partners))

    head_copies = []
    for k in range(1, n_head):
        to = head_at(k)
        copy = send(
            kvs.at[:, :, pl.ds(pl.multiple_of(to * DH, DH), DH)],
            kvb.at[0, :, pl.ds(pl.multiple_of(g * slot_rows, slot_rows), slot_rows), :],
            head_s.at[k], head_r.at[k], (c, to),
        )
        copy.start()
        head_copies.append(copy)
    kvb[0, :, pl.ds(pl.multiple_of(g * slot_rows, slot_rows), slot_rows), :] = kvs[
        :, :, pl.ds(pl.multiple_of(g * DH, DH), DH)
    ]

    pad16[...] = jnp.zeros_like(pad16)
    pad16[0:PER_GROUP, :] = ld[...]
    cum = triangle_sum(pad16[...], (row_at <= col_at).astype(F32).astype(BF16))
    cum_row[...] = cum
    cum_t = jnp.concatenate([cum, jnp.zeros((DH - 16, ROWS), F32)], axis=0).T
    carry_rows = []
    for h in range(PER_GROUP):
        lanes = slice(h * DH, (h + 1) * DH)
        col = cum_t[:, h : h + 1]
        final_cum = col[ROWS - 1 : ROWS, :]
        last = jnp.where(pos_col >= start_last, jnp.exp(final_cum - col), 0.0)
        first = jnp.where(start_col < 0.0, jnp.exp(col), 0.0) * SCALING
        cum_col[h] = jnp.broadcast_to(col, (ROWS, DH))
        last = jnp.broadcast_to(last, (ROWS, DH))
        first = jnp.broadcast_to(first, (ROWS, DH))
        last_w[h] = last
        first_w[h] = first
        keys_w = (last * rk[:, lanes].astype(F32)).astype(BF16)
        queries_w = (first * rq[:, lanes].astype(F32)).astype(BF16)
        own_f[h * DH : (h + 1) * DH, :] = matmul_tn(keys_w, rv[:, lanes])
        own_b[h * DH : (h + 1) * DH, :] = matmul_tn(queries_w, rg[:, lanes])
        carry = jnp.where(start_last < 0.0, jnp.exp(final_cum), 0.0)
        carry_rows.append(jnp.broadcast_to(carry, (8, DH)))
    which = lax.broadcasted_iota(jnp.int32, (8, DH), 0)
    carries = jnp.zeros((8, DH), F32)
    for h in range(PER_GROUP):
        carries = jnp.where(which == h, carry_rows[h], carries)
    own_f[PER_GROUP * DH :, :] = carries
    own_b[PER_GROUP * DH :, :] = carries

    for i in range(TILES):
        for h in range(PER_GROUP):
            at = (i * PER_GROUP + h) * TILE
            qs[at : at + TILE, :] = cq[i * TILE : (i + 1) * TILE, h * DH : (h + 1) * DH]
            os[at : at + TILE, :] = cg[i * TILE : (i + 1) * TILE, h * DH : (h + 1) * DH]

    for copy in head_copies:
        copy.wait_recv()
    kv_copies = [
        send(kvb.at[0], kvb.at[1], kv_s.at[0], kv_r.at[0], (ctx_at(1), g)),
        send(kvb.at[0], kvb.at[3], kv_s.at[1], kv_r.at[1], (ctx_at(3), g)),
        send(kvb.at[1, 0], kvb.at[2, 0], kv_s.at[2], kv_r.at[2], (ctx_at(1), g)),
        send(kvb.at[3, 1], kvb.at[2, 1], kv_s.at[3], kv_r.at[3], (ctx_at(-1), g)),
    ]
    state_copies = [
        send(own_f, got_f.at[0], st_s.at[0], st_r.at[0], (ctx_at(1), g)),
        send(own_b, got_b.at[0], st_s.at[1], st_r.at[1], (ctx_at(-1), g)),
        send(own_f, got_f.at[2], st_s.at[2], st_r.at[2], (ctx_at(3), g)),
        send(own_b, got_b.at[2], st_s.at[3], st_r.at[3], (ctx_at(-3), g)),
        send(got_f.at[0], got_f.at[1], st_s.at[4], st_r.at[4], (ctx_at(1), g)),
        send(got_b.at[0], got_b.at[1], st_s.at[5], st_r.at[5], (ctx_at(-1), g)),
    ]
    kv_copies[0].start()
    kv_copies[1].start()

    tile_row = lax.broadcasted_iota(jnp.int32, (TILE, TILE), 0)
    tile_col = lax.broadcasted_iota(jnp.int32, (TILE, TILE), 1)
    tile_pos = tile_row.astype(F32)
    causal = tile_row <= tile_col

    def retention_head(h, nothing):
        lanes = pl.ds(pl.multiple_of(h * DH, DH), DH)
        for ti in range(TILES):
            t = slice(ti * TILE, (ti + 1) * TILE)
            rq_t = rq[t, lanes]
            rg_t = rg[t, lanes]
            cum_t_row = cum_row[pl.ds(h, 1), t]
            query_t = jnp.zeros((DH, TILE), F32)
            for si in range(ti + 1):
                s = slice(si * TILE, (si + 1) * TILE)
                rk_s = rk[s, lanes]
                allowed = tile_pos >= start_row[0:1, t] - float(si * TILE)
                if si == ti:
                    allowed = allowed & causal
                gap = jnp.minimum(cum_t_row - cum_col[h, s, 0:1], 0.0)
                within = jnp.where(allowed, jnp.exp(gap) * SCALING, 0.0)
                grad_w = (within * matmul_nt(rv[s, lanes], rg_t)).astype(BF16)
                score_w = (within * matmul_nt(rk_s, rq_t)).astype(BF16)
                query_t = query_t + matmul_tn(rk_s, grad_w)
                key_term = matmul(grad_w, rq_t)
                value_term = matmul(score_w, rg_t)
                if si == ti:
                    kf[h, s, :] = key_term
                    vf[h, s, :] = value_term
                else:
                    kf[h, s, :] = kf[h, s, :] + key_term
                    vf[h, s, :] = vf[h, s, :] + value_term
            qf[h, t, :] = query_t.T

        @pl.when(h == 1)
        def _():
            kv_copies[0].wait_recv()
            kv_copies[2].start()
            kv_copies[1].wait_recv()
            kv_copies[3].start()
            for copy in state_copies[:4]:
                copy.start()

        return nothing

    lax.fori_loop(0, PER_GROUP, retention_head, 0)

    kv_copies[2].wait_recv()
    kv_copies[3].wait_recv()
    for d in range(4):
        kt[d] = kvb[d, 0].astype(F32).T.astype(BF16)

    def attention_head(h, nothing):
        for i in range(TILES):
            cols = pl.ds(pl.multiple_of(i * (PER_GROUP * TILE) + h * TILE, TILE), TILE)
            query = qs[cols, :]
            upstream = os[cols, :]
            start_t = start_row[0:1, i * TILE : (i + 1) * TILE]
            pieces = [(0, j) for j in range(i + 1)]
            pieces += [(d, j) for d in (1, 2) for j in range(TILES)]
            pieces += [(3, j) for j in range(i, TILES)]
            top = jnp.full((1, TILE), -1e30, F32)
            for n, (d, j) in enumerate(pieces):
                s = slice(j * TILE, (j + 1) * TILE)
                raw = matmul_nt(kvb[d, 0, s, :], query)
                allowed = tile_pos >= start_t + float(d * ROWS - j * TILE)
                if d == 0 and j == i:
                    allowed = allowed & causal
                raw = jnp.where(allowed, raw, -1e30)
                score[n * TILE : (n + 1) * TILE, :] = raw
                top = jnp.maximum(top, jnp.max(raw, axis=0, keepdims=True))
            total = jnp.zeros((1, TILE), F32)
            for n in range(len(pieces)):
                at = slice(n * TILE, (n + 1) * TILE)
                term = jnp.exp2((score[at, :] - top) * EXPONENT_SCALE)
                score[at, :] = term
                total = total + jnp.sum(term, axis=0, keepdims=True)
            inverse = 1.0 / total
            row_dot = jnp.zeros((1, TILE), F32)
            for n, (d, j) in enumerate(pieces):
                s = slice(j * TILE, (j + 1) * TILE)
                at = slice(n * TILE, (n + 1) * TILE)
                weights = score[at, :] * inverse
                weights_b = weights.astype(BF16)
                dweights = matmul_nt(kvb[d, 1, s, :], upstream)
                score[at, :] = weights
                dprob[at, :] = dweights
                prob_t[d, s, cols] = weights_b
                row_dot = row_dot + jnp.sum(weights_b.astype(F32) * dweights, axis=0, keepdims=True)
            query_t = jnp.zeros((DH, TILE), F32)
            for n, (d, j) in enumerate(pieces):
                s = slice(j * TILE, (j + 1) * TILE)
                at = slice(n * TILE, (n + 1) * TILE)
                dscores_b = (score[at, :] * (dprob[at, :] - row_dot)).astype(BF16)
                dscore_t[d, s, cols] = dscores_b
                query_t = query_t + matmul(kt[d, :, s], dscores_b)
            gq[i * TILE : (i + 1) * TILE, pl.ds(pl.multiple_of(h * DH, DH), DH)] = (
                query_t.T * SCALING
            ).astype(BF16)

        @pl.when(h == 0)
        def _():
            state_copies[0].wait_recv()
            state_copies[4].start()
            state_copies[1].wait_recv()
            state_copies[5].start()

        return nothing

    lax.fori_loop(0, PER_GROUP, attention_head, 0)

    width = PER_GROUP * TILE

    def partial_grads(d, j):
        s = slice(j * TILE, (j + 1) * TILE)
        cols = slice(0, TILES * width)
        if d == 0:
            cols = slice(j * width, TILES * width)
        if d == 3:
            cols = slice(0, (j + 1) * width)
        keys = matmul(dscore_t[d, s, cols], qs[cols, :]) * SCALING
        values = matmul(prob_t[d, s, cols], os[cols, :])
        return keys, values

    grad_copies = [
        send(part.at[1, 0], half.at[0], gr_s.at[0], gr_r.at[0], (ctx_at(-1), g)),
        send(part.at[1, 1], half.at[1], gr_s.at[1], gr_r.at[1], (ctx_at(1), g)),
        send(part.at[2], back.at[1], gr_s.at[2], gr_r.at[2], (ctx_at(-3), g)),
        send(part.at[0], back.at[0], gr_s.at[3], gr_r.at[3], (ctx_at(-1), g)),
    ]
    tiles = [slice(j * TILE, (j + 1) * TILE) for j in range(TILES)]
    for j in range(TILES):
        keys, values = partial_grads(2, j)
        part[1, 0, tiles[j], :] = keys.astype(BF16)
        part[1, 1, tiles[j], :] = values.astype(BF16)
    grad_copies[0].start()
    grad_copies[1].start()
    third = [partial_grads(3, j) for j in range(TILES)]
    for j in range(TILES):
        part[2, 0, tiles[j], :] = third[j][0].astype(BF16)
        home[1, tiles[j], :] = third[j][1]
    grad_copies[1].wait_recv()
    part[2, 1] = (home[1] + half[1].astype(F32)).astype(BF16)
    grad_copies[2].start()
    for j in range(TILES):
        keys, values = partial_grads(1, j)
        home[0, tiles[j], :] = keys
        part[0, 1, tiles[j], :] = values.astype(BF16)
    grad_copies[0].wait_recv()
    part[0, 0] = (home[0] + half[0].astype(F32)).astype(BF16)
    grad_copies[3].start()
    for j in range(TILES):
        keys, values = partial_grads(0, j)
        home[0, tiles[j], :] = keys
        home[1, tiles[j], :] = values

    for copy in state_copies[2:]:
        copy.wait_recv()
    sums = jnp.zeros((ROWS, DH), F32)
    lane_at = lax.broadcasted_iota(jnp.int32, (ROWS, DH), 1)
    for h in range(PER_GROUP):
        lanes = slice(h * DH, (h + 1) * DH)
        block = slice(h * DH, (h + 1) * DH)
        carry_at = slice(PER_GROUP * DH + h, PER_GROUP * DH + h + 1)

        def chained(got):
            inner = got[1, block, :] + got[1, carry_at, :] * got[2, block, :]
            return (got[0, block, :] + got[0, carry_at, :] * inner).astype(BF16)

        state_b = jnp.where(c > 0, chained(got_f), jnp.zeros((DH, DH), BF16))
        later_b = jnp.where(c < n_ctx - 1, chained(got_b), jnp.zeros((DH, DH), BF16))
        last = last_w[h]
        query_f = qf[h] + first_w[h] * matmul_nt(rg[:, lanes], state_b)
        key_f = kf[h] + last * matmul_nt(rv[:, lanes], later_b)
        value_f = vf[h] + last * matmul(rk[:, lanes], later_b)
        oq[:, lanes] = query_f.astype(BF16)
        ok[:, lanes] = key_f.astype(BF16)
        ov[:, lanes] = value_f.astype(BF16)
        residue = jnp.sum(rq[:, lanes].astype(F32) * query_f, axis=1, keepdims=True) - jnp.sum(
            rk[:, lanes].astype(F32) * key_f, axis=1, keepdims=True
        )
        sums = jnp.where(lane_at == h, residue, sums)
    suffix = triangle_sum(sums.T[0:16], (row_at >= col_at).astype(F32).astype(BF16))
    cum_row[...] = suffix
    tot_x[0] = jnp.broadcast_to(suffix[0:8, 0:1], (8, DH))
    x_copies = [
        send(tot_x.at[0], tot_x.at[k], tx_s.at[k], tx_r.at[k], (x_peer(k), g))
        for k in range(1, X_RING)
    ]
    for copy in x_copies:
        copy.start()

    grad_copies[2].wait_recv()
    grad_copies[3].wait_recv()
    for m in range(2):
        total = home[m] + back[0, m].astype(F32) + back[1, m].astype(F32)
        final[m] = total.astype(BF16)
    final_copies = []
    for k in range(1, n_head):
        to = head_at(k)
        copy = send(
            final.at[:, pl.ds(pl.multiple_of(to * slot_rows, slot_rows), slot_rows), :],
            landed.at[:, :, pl.ds(pl.multiple_of(g * DH, DH), DH)],
            fin_s.at[k], fin_r.at[k], (c, to),
        )
        copy.start()
        final_copies.append(copy)
    landed[:, :, pl.ds(pl.multiple_of(g * DH, DH), DH)] = final[
        :, pl.ds(pl.multiple_of(g * slot_rows, slot_rows), slot_rows), :
    ]

    for copy in x_copies:
        copy.wait_recv()
    row_total = tot_x[0]
    tail = jnp.zeros((8, DH), F32)
    for k in range(1, X_RING):
        row_total = row_total + tot_x[k]
        tail = tail + jnp.where(lax.rem(x - k + X_RING, X_RING) > x, tot_x[k], 0.0)
    tot_z[0] = row_total
    z_copies = [
        send(tot_z.at[0], tot_z.at[k], tz_s.at[k], tz_r.at[k], (z_peer(k), g))
        for k in range(1, z_ring)
    ]
    for copy in z_copies:
        copy.start()
    for copy in z_copies:
        copy.wait_recv()
    for k in range(1, z_ring):
        tail = tail + jnp.where(lax.rem(z - k + z_ring, z_ring) > z, tot_z[k], 0.0)
    dg[...] = (cum_row[0:8, :] + tail[:, 0:1])[0:PER_GROUP]

    for copy in final_copies:
        copy.wait_recv()
    gk[...] = landed[0]
    gv[...] = landed[1]
    for copy in (
        head_copies + kv_copies + state_copies + grad_copies + final_copies + x_copies + z_copies
    ):
        copy.wait_send()


def on_device(
    cross_query, cross_grad, cache_keys, cache_values, retention_query, retention_key,
    retention_value, retention_grad, log_decay, doc_offsets,
):
    n_ctx = lax.axis_size("ctx")
    n_head = lax.axis_size("head")
    wide = jax.ShapeDtypeStruct(cross_query.shape, BF16)
    cache = jax.ShapeDtypeStruct(cache_keys.shape, BF16)
    vmem = pl.BlockSpec(memory_space=pltpu.VMEM)
    slot_rows, all_heads = cache_keys.shape
    dma = pltpu.SemaphoreType.DMA
    heads_wide = pltpu.VMEM((PER_GROUP, ROWS, DH), F32)
    return pl.pallas_call(
        lambda *refs: body(n_ctx, n_head, *refs),
        out_shape=(
            wide, cache, cache, wide, wide, wide, jax.ShapeDtypeStruct(log_decay.shape, F32),
        ),
        in_specs=[vmem] * 10,
        out_specs=(vmem,) * 7,
        scratch_shapes=[
            pltpu.VMEM((2, slot_rows, all_heads), BF16),
            pltpu.VMEM((4, 2, ROWS, DH), BF16),
            pltpu.VMEM((STATE_ROWS, DH), F32),
            pltpu.VMEM((STATE_ROWS, DH), F32),
            pltpu.VMEM((3, STATE_ROWS, DH), F32),
            pltpu.VMEM((3, STATE_ROWS, DH), F32),
            pltpu.VMEM((3, 2, ROWS, DH), BF16),
            pltpu.VMEM((2, ROWS, DH), BF16),
            pltpu.VMEM((2, 2, ROWS, DH), BF16),
            pltpu.VMEM((2, ROWS, DH), F32),
            pltpu.VMEM((2, ROWS, DH), BF16),
            pltpu.VMEM((2, slot_rows, all_heads), BF16),
            pltpu.VMEM((X_RING, 8, DH), F32),
            pltpu.VMEM((max(n_ctx // X_RING, 1), 8, DH), F32),
            pltpu.VMEM((PER_GROUP * ROWS, DH), BF16),
            pltpu.VMEM((PER_GROUP * ROWS, DH), BF16),
            pltpu.VMEM((4, DH, ROWS), BF16),
            pltpu.VMEM((7 * TILE, TILE), F32),
            pltpu.VMEM((7 * TILE, TILE), F32),
            pltpu.VMEM((4, ROWS, PER_GROUP * ROWS), BF16),
            pltpu.VMEM((4, ROWS, PER_GROUP * ROWS), BF16),
            pltpu.VMEM((8, ROWS), F32),
            pltpu.VMEM((16, ROWS), F32),
            heads_wide,
            heads_wide,
            heads_wide,
            heads_wide,
            heads_wide,
            heads_wide,
            pltpu.VMEM((16, ROWS), F32),
            dma((8,)), dma((8,)), dma((4,)), dma((4,)), dma((6,)), dma((6,)), dma((4,)), dma((4,)),
            dma((8,)), dma((8,)), dma((4,)), dma((4,)), dma((8,)), dma((8,)),
        ],
        compiler_params=pltpu.CompilerParams(
            collective_id=0, has_side_effects=True, vmem_limit_bytes=56 * 1024 * 1024
        ),
    )(
        cross_query, cross_grad, cache_keys, cache_values, retention_query, retention_key,
        retention_value, retention_grad, log_decay, doc_offsets.reshape(1, -1),
    )


def solution(mesh):
    wide = P("ctx", "head")
    cache = P(("ctx", "head"), None)
    return jax.shard_map(
        on_device,
        mesh=mesh,
        in_specs=(wide, wide, cache, cache, wide, wide, wide, wide, P("head", "ctx"), P()),
        out_specs=(wide, cache, cache, wide, wide, wide, P("head", "ctx")),
        check_vma=False,
    )
```

time: 928 us -> 82.5 us (0.09)
  the two profiles are of different devices: /device:TPU:103 before, /device:TPU:3 now
where the time goes in v2:
time: 82.5 us; the launch traced here: 82.3 us
  Pallas kernels  74.8 us (91%)
  local copies, waits for them, and re-layouts  6.77 us (8%)
    pallas_call x1, Pallas kernels, on_device(): pl.pallas_call(lambda *refs: body(n_ctx, n_head, *refs), out_shape=(wide,...  74.8 us
    unnamed x19, local copies, waits for them, and re-layouts  6.77 us

profile of v2, /device:TPU:3, one launch (start us, length us, event | category | flops | bytes accessed | tf_op | source)
XLA Modules:
  0.0 82.3 jit_solution(14577273830850779789)
XLA Ops:
  0.6 74.8 %shard_map.153 = (bf16[512,384]{1,0:T(8,128)(2,1)}, bf16[64,1024]{1,0:T(8,128)(2,1)}, bf16[64,1024]{1,0:T(8,128)(2,1)}, bf16[512,384]{1,0:T(8,128)(2,1)}, bf16[5...) custom-call(bf16[512,384]{1,0:T(8,128)(2,1)} %refs_0_.1, bf16[512,384]{1,0:T(8,128)(2,1)} %refs_1_.1, ...), custom_call_target="tpu_custom_call" | custom-call | tf_op jit(solution)/shard_map/pallas_call | solution.py:428
  75.5 0.0 copy-start.4
  75.5 0.0 copy-start.3
  75.5 1.8 %copy.24 = bf16[512,384]{1,0:T(8,128)(2,1)} copy(bf16[512,384]{1,0:T(8,128)(2,1)} %get-tuple-element.14) | data formatting | bytes 786432
  77.3 0.0 copy-done.4
  77.3 0.0 copy-start.2
  77.3 0.7 copy.25
  78.0 0.0 copy-done.3
  78.0 0.7 copy.26
  78.6 0.0 copy-done.2
  78.6 0.0 copy-start.1
  78.6 0.7 copy.27
  79.4 0.4 copy-done.1
  79.8 0.0 copy-start
  79.8 0.7 copy.28
  80.5 0.4 copy-done
  80.9 0.0 copy-start.5
  80.9 0.7 copy.29
  81.7 0.0 copy-done.5
  81.7 0.6 copy.30
Async XLA Ops:
  75.5 1.8 %copy-start.4 = (bf16[64,1024]{1,0:T(8,128)(2,1)S(1)}, bf16[64,1024]{1,0:T(8,128)(2,1)}, u32[]{:S(2)}) copy-start(bf16[64,1024]{1,0:T(8,128)(2,1)} %get-tuple-element.15) | copy-start | bytes 393220
  75.5 2.5 %copy-start.3 = (bf16[64,1024]{1,0:T(8,128)(2,1)S(1)}, bf16[64,1024]{1,0:T(8,128)(2,1)}, u32[]{:S(2)}) copy-start(bf16[64,1024]{1,0:T(8,128)(2,1)} %get-tuple-element.16) | copy-start | bytes 393220
  77.3 1.3 %copy-start.2 = (bf16[512,384]{1,0:T(8,128)(2,1)S(1)}, bf16[512,384]{1,0:T(8,128)(2,1)}, u32[]{:S(2)}) copy-start(bf16[512,384]{1,0:T(8,128)(2,1)} %get-tuple-element.17) | copy-start | bytes 1179652
  78.6 1.1 %copy-start.1 = (bf16[512,384]{1,0:T(8,128)(2,1)S(1)}, bf16[512,384]{1,0:T(8,128)(2,1)}, u32[]{:S(2)}) copy-start(bf16[512,384]{1,0:T(8,128)(2,1)} %get-tuple-element.18) | copy-start | bytes 1179652
  79.8 1.1 %copy-start = (bf16[512,384]{1,0:T(8,128)(2,1)S(1)}, bf16[512,384]{1,0:T(8,128)(2,1)}, u32[]{:S(2)}) copy-start(bf16[512,384]{1,0:T(8,128)(2,1)} %get-tuple-element.19) | copy-start | bytes 1179652
  80.9 0.8 copy-start.5

commit v3 on v2

--- a/solution.py
+++ b/solution.py
@@ -50,10 +50,10 @@
     n_ctx, n_head,
     cq, cg, ck, cv, rq, rk, rv, rg, ld, offs,
     gq, gk, gv, oq, ok, ov, dg,
-    kvs, kvb, own_f, own_b, got_f, got_b, part, half, back, home, final, landed, tot_x, tot_z,
+    kvs, kvb, own_f, own_b, got_f, got_b, part, half, back, home, wait_sum, final, landed, tot_x, tot_z,
     qs, os, kt, score, dprob, prob_t, dscore_t,
     start_row, cum_row, cum_col, last_w, first_w, qf, kf, vf, pad16,
-    head_s, head_r, kv_s, kv_r, st_s, st_r, gr_s, gr_r, fin_s, fin_r, tx_s, tx_r, tz_s, tz_r,
+    head_s, head_r, kv_s, kv_r, st_s, st_r, gr_s, gr_r, fin_s, fin_r, tx_s, tx_r, tz_s, tz_r, ready,
 ):
     c = lax.axis_index("ctx")
     g = lax.axis_index("head")
@@ -73,7 +73,7 @@
         return z * X_RING + lax.rem(x + offset, X_RING)
 
     def z_peer(offset):
-        return lax.rem(z + offset, z_ring) * X_RING + x
+        return lax.rem(z + (offset + z_ring), z_ring) * X_RING + x
 
     def send(src, dst, send_sem, recv_sem, device):
         return pltpu.make_async_remote_copy(
@@ -81,13 +81,70 @@
             device_id=device, device_id_type=MESH,
         )
 
-    partners = [(c, head_at(k)) for k in range(1, n_head)]
-    partners += [(ctx_at(k), g) for k in (1, -1, 3, -3)]
-    partners += [(x_peer(k), g) for k in range(1, X_RING)]
-    partners += [(z_peer(k), g) for k in range(1, z_ring)]
+    def has(offset):
+        if offset > 0:
+            return c < n_ctx - offset
+        return c >= -offset
+
+    def z_has(offset):
+        if offset > 0:
+            return z < z_ring - offset
+        return z >= -offset
+
+    def start(transfer):
+        pl.when(transfer[1])(lambda: transfer[0].start())
+
+    def receive(transfer):
+        pl.when(transfer[2])(lambda: transfer[0].wait_recv())
+
+    def sent(transfer):
+        pl.when(transfer[1])(lambda: transfer[0].wait_send())
+
+    def clear(condition, ref):
+        @pl.when(condition)
+        def _():
+            ref[...] = jnp.zeros(ref.shape, ref.dtype)
+
     barrier = pltpu.get_barrier_semaphore()
-    for device in partners:
-        pl.semaphore_signal(barrier, inc=1, device_id=device, device_id_type=MESH)
+    greetings = n_head - 1 + X_RING - 1
+    for k in range(1, n_head):
+        pl.semaphore_signal(barrier, inc=1, device_id=(c, head_at(k)), device_id_type=MESH)
+    for k in range(1, X_RING):
+        pl.semaphore_signal(barrier, inc=1, device_id=(x_peer(k), g), device_id_type=MESH)
+    for k in (1, -1, 3, -3):
+        @pl.when(has(k))
+        def _():
+            pl.semaphore_signal(barrier, inc=1, device_id=(ctx_at(k), g), device_id_type=MESH)
+
+        greetings = greetings + has(k).astype(jnp.int32)
+    for k in (1, -1):
+        if z_ring > 1:
+            @pl.when(z_has(k))
+            def _():
+                pl.semaphore_signal(barrier, inc=1, device_id=(z_peer(k), g), device_id_type=MESH)
+
+            greetings = greetings + z_has(k).astype(jnp.int32)
+
+    def ready_round(r):
+        if r < z_ring - 1:
+            if r > 1:
+                pl.when(z >= r)(lambda: pl.semaphore_wait(ready.at[r - 1], 1))
+
+            @pl.when((z >= r) & (z < z_ring - 1))
+            def _():
+                pl.semaphore_signal(
+                    ready.at[r], inc=1, device_id=(z_peer(1), g), device_id_type=MESH
+                )
+
+    for d in (1, 2, 3):
+        clear(c < d, kvb.at[d])
+        clear(c < d, got_f.at[d - 1])
+        clear(c >= n_ctx - d, got_b.at[d - 1])
+    clear((c == 0) | (c == n_ctx - 1), half.at[0])
+    clear(c < 3, half.at[1])
+    clear(c != n_ctx - 2, half.at[2])
+    clear(c >= n_ctx - 1, back.at[0])
+    clear(c >= n_ctx - 3, back.at[1])
 
     kvs[0] = ck[...]
     kvs[1] = cv[...]
@@ -101,7 +158,12 @@
     row_at = lax.broadcasted_iota(jnp.int32, (ROWS, ROWS), 0)
     col_at = lax.broadcasted_iota(jnp.int32, (ROWS, ROWS), 1)
 
-    pl.semaphore_wait(barrier, len(partners))
+    pad16[...] = jnp.zeros_like(pad16)
+    pad16[0:PER_GROUP, :] = ld[...]
+    cum = triangle_sum(pad16[...], (row_at <= col_at).astype(F32).astype(BF16))
+    cum_row[...] = cum
+    cum_t = jnp.concatenate([cum, jnp.zeros((DH - 16, ROWS), F32)], axis=0).T
+    pl.semaphore_wait(barrier, greetings)
 
     head_copies = []
     for k in range(1, n_head):
@@ -117,11 +179,8 @@
         :, :, pl.ds(pl.multiple_of(g * DH, DH), DH)
     ]
 
-    pad16[...] = jnp.zeros_like(pad16)
-    pad16[0:PER_GROUP, :] = ld[...]
-    cum = triangle_sum(pad16[...], (row_at <= col_at).astype(F32).astype(BF16))
-    cum_row[...] = cum
-    cum_t = jnp.concatenate([cum, jnp.zeros((DH - 16, ROWS), F32)], axis=0).T
+    ready_round(1)
+
     carry_rows = []
     for h in range(PER_GROUP):
         lanes = slice(h * DH, (h + 1) * DH)
@@ -147,30 +206,43 @@
     own_f[PER_GROUP * DH :, :] = carries
     own_b[PER_GROUP * DH :, :] = carries
 
+    for copy in head_copies:
+        copy.wait_recv()
+    up, down = (ctx_at(1), g), (ctx_at(-1), g)
+    far_up, far_down = (ctx_at(3), g), (ctx_at(-3), g)
+
+    def transfer(sems, n, src, dst, device, sends, receives):
+        return send(src, dst, sems[0].at[n], sems[1].at[n], device), sends, receives
+
+    kv_sems, st_sems, gr_sems = (kv_s, kv_r), (st_s, st_r), (gr_s, gr_r)
+    kv_copies = [
+        transfer(kv_sems, 0, kvb.at[0, 0], kvb.at[1, 0], up, has(1), has(-1)),
+        transfer(kv_sems, 1, kvb.at[0, 1], kvb.at[3, 1], far_up, has(3), has(-3)),
+        transfer(kv_sems, 2, kvb.at[0, 1], kvb.at[1, 1], up, has(1), has(-1)),
+        transfer(kv_sems, 3, kvb.at[0, 0], kvb.at[3, 0], far_up, has(3), has(-3)),
+        transfer(kv_sems, 4, kvb.at[1, 0], kvb.at[2, 0], up, has(1) & has(-1), has(-2)),
+        transfer(
+            kv_sems, 5, kvb.at[3, 1], kvb.at[2, 1], down, has(-3), (c >= 2) & (c < n_ctx - 1)
+        ),
+        transfer(kv_sems, 6, kvb.at[1, 1], kvb.at[2, 1], up, c == n_ctx - 2, c == n_ctx - 1),
+    ]
+    state_copies = [
+        transfer(st_sems, 0, own_f, got_f.at[0], up, has(1), has(-1)),
+        transfer(st_sems, 1, own_b, got_b.at[0], down, has(-1), has(1)),
+        transfer(st_sems, 2, own_f, got_f.at[2], far_up, has(3), has(-3)),
+        transfer(st_sems, 3, own_b, got_b.at[2], far_down, has(-3), has(3)),
+        transfer(st_sems, 4, got_f.at[0], got_f.at[1], up, has(1) & has(-1), has(-2)),
+        transfer(st_sems, 5, got_b.at[0], got_b.at[1], down, has(1) & has(-1), has(2)),
+    ]
+    for copy in kv_copies[:4]:
+        start(copy)
+    ready_round(2)
+
     for i in range(TILES):
         for h in range(PER_GROUP):
             at = (i * PER_GROUP + h) * TILE
             qs[at : at + TILE, :] = cq[i * TILE : (i + 1) * TILE, h * DH : (h + 1) * DH]
             os[at : at + TILE, :] = cg[i * TILE : (i + 1) * TILE, h * DH : (h + 1) * DH]
-
-    for copy in head_copies:
-        copy.wait_recv()
-    kv_copies = [
-        send(kvb.at[0], kvb.at[1], kv_s.at[0], kv_r.at[0], (ctx_at(1), g)),
-        send(kvb.at[0], kvb.at[3], kv_s.at[1], kv_r.at[1], (ctx_at(3), g)),
-        send(kvb.at[1, 0], kvb.at[2, 0], kv_s.at[2], kv_r.at[2], (ctx_at(1), g)),
-        send(kvb.at[3, 1], kvb.at[2, 1], kv_s.at[3], kv_r.at[3], (ctx_at(-1), g)),
-    ]
-    state_copies = [
-        send(own_f, got_f.at[0], st_s.at[0], st_r.at[0], (ctx_at(1), g)),
-        send(own_b, got_b.at[0], st_s.at[1], st_r.at[1], (ctx_at(-1), g)),
-        send(own_f, got_f.at[2], st_s.at[2], st_r.at[2], (ctx_at(3), g)),
-        send(own_b, got_b.at[2], st_s.at[3], st_r.at[3], (ctx_at(-3), g)),
-        send(got_f.at[0], got_f.at[1], st_s.at[4], st_r.at[4], (ctx_at(1), g)),
-        send(got_b.at[0], got_b.at[1], st_s.at[5], st_r.at[5], (ctx_at(-1), g)),
-    ]
-    kv_copies[0].start()
-    kv_copies[1].start()
 
     tile_row = lax.broadcasted_iota(jnp.int32, (TILE, TILE), 0)
     tile_col = lax.broadcasted_iota(jnp.int32, (TILE, TILE), 1)
@@ -206,23 +278,25 @@
                     vf[h, s, :] = vf[h, s, :] + value_term
             qf[h, t, :] = query_t.T
 
-        @pl.when(h == 1)
-        def _():
-            kv_copies[0].wait_recv()
-            kv_copies[2].start()
-            kv_copies[1].wait_recv()
-            kv_copies[3].start()
-            for copy in state_copies[:4]:
-                copy.start()
-
         return nothing
 
     lax.fori_loop(0, PER_GROUP, retention_head, 0)
 
-    kv_copies[2].wait_recv()
-    kv_copies[3].wait_recv()
-    for d in range(4):
+    for n in (0, 1):
+        receive(kv_copies[n])
+    start(kv_copies[4])
+    start(kv_copies[5])
+    receive(kv_copies[2])
+    start(kv_copies[6])
+    receive(kv_copies[3])
+    ready_round(3)
+    for d in (0, 1, 3):
         kt[d] = kvb[d, 0].astype(F32).T.astype(BF16)
+    for n in (4, 5, 6):
+        receive(kv_copies[n])
+    kt[2] = kvb[2, 0].astype(F32).T.astype(BF16)
+    start(state_copies[0])
+    start(state_copies[1])
 
     def attention_head(h, nothing):
         for i in range(TILES):
@@ -274,10 +348,17 @@
 
         @pl.when(h == 0)
         def _():
-            state_copies[0].wait_recv()
-            state_copies[4].start()
-            state_copies[1].wait_recv()
-            state_copies[5].start()
+            start(state_copies[2])
+            start(state_copies[3])
+            ready_round(4)
+
+        @pl.when(h == 1)
+        def _():
+            receive(state_copies[0])
+            start(state_copies[4])
+            receive(state_copies[1])
+            start(state_copies[5])
+            ready_round(5)
 
         return nothing
 
@@ -285,51 +366,58 @@
 
     width = PER_GROUP * TILE
 
-    def partial_grads(d, j):
-        s = slice(j * TILE, (j + 1) * TILE)
+    def partial_at(d, j):
         cols = slice(0, TILES * width)
         if d == 0:
             cols = slice(j * width, TILES * width)
         if d == 3:
             cols = slice(0, (j + 1) * width)
-        keys = matmul(dscore_t[d, s, cols], qs[cols, :]) * SCALING
-        values = matmul(prob_t[d, s, cols], os[cols, :])
-        return keys, values
-
+        return slice(j * TILE, (j + 1) * TILE), cols
+
+    middle_device = has(1) & has(-1)
     grad_copies = [
-        send(part.at[1, 0], half.at[0], gr_s.at[0], gr_r.at[0], (ctx_at(-1), g)),
-        send(part.at[1, 1], half.at[1], gr_s.at[1], gr_r.at[1], (ctx_at(1), g)),
-        send(part.at[2], back.at[1], gr_s.at[2], gr_r.at[2], (ctx_at(-3), g)),
-        send(part.at[0], back.at[0], gr_s.at[3], gr_r.at[3], (ctx_at(-1), g)),
+        transfer(gr_sems, 0, part.at[1, 0], half.at[0], down, has(-2), middle_device),
+        transfer(gr_sems, 1, part.at[1, 1], half.at[1], up, has(-2) & has(1), has(-3)),
+        transfer(gr_sems, 2, part.at[1, 1], half.at[2], down, c == n_ctx - 1, c == n_ctx - 2),
+        transfer(gr_sems, 3, part.at[2, 0], back.at[1, 0], far_down, has(-3), has(3)),
+        transfer(gr_sems, 4, part.at[0, 1], back.at[0, 1], down, has(-1), has(1)),
+        transfer(gr_sems, 5, part.at[2, 1], back.at[1, 1], far_down, has(-3), has(3)),
+        transfer(gr_sems, 6, part.at[0, 0], back.at[0, 0], down, has(-1), has(1)),
     ]
-    tiles = [slice(j * TILE, (j + 1) * TILE) for j in range(TILES)]
-    for j in range(TILES):
-        keys, values = partial_grads(2, j)
-        part[1, 0, tiles[j], :] = keys.astype(BF16)
-        part[1, 1, tiles[j], :] = values.astype(BF16)
-    grad_copies[0].start()
-    grad_copies[1].start()
-    third = [partial_grads(3, j) for j in range(TILES)]
-    for j in range(TILES):
-        part[2, 0, tiles[j], :] = third[j][0].astype(BF16)
-        home[1, tiles[j], :] = third[j][1]
-    grad_copies[1].wait_recv()
-    part[2, 1] = (home[1] + half[1].astype(F32)).astype(BF16)
-    grad_copies[2].start()
-    for j in range(TILES):
-        keys, values = partial_grads(1, j)
-        home[0, tiles[j], :] = keys
-        part[0, 1, tiles[j], :] = values.astype(BF16)
-    grad_copies[0].wait_recv()
-    part[0, 0] = (home[0] + half[0].astype(F32)).astype(BF16)
-    grad_copies[3].start()
-    for j in range(TILES):
-        keys, values = partial_grads(0, j)
-        home[0, tiles[j], :] = keys
-        home[1, tiles[j], :] = values
+
+    def key_grad(d, out, at):
+        for j in range(TILES):
+            s, cols = partial_at(d, j)
+            value = matmul(dscore_t[d, s, cols], qs[cols, :]) * SCALING
+            out[at + (s,)] = value.astype(out.dtype)
+
+    def value_grad(d, out, at):
+        for j in range(TILES):
+            s, cols = partial_at(d, j)
+            value = matmul(prob_t[d, s, cols], os[cols, :])
+            out[at + (s,)] = value.astype(out.dtype)
+
+    key_grad(2, part, (1, 0))
+    start(grad_copies[0])
+    value_grad(2, part, (1, 1))
+    start(grad_copies[1])
+    start(grad_copies[2])
+    key_grad(3, part, (2, 0))
+    start(grad_copies[3])
+    value_grad(1, wait_sum, (0,))
+
+    receive(grad_copies[2])
+
+    part[0, 1] = (wait_sum[0] + half[2].astype(F32)).astype(BF16)
+    start(grad_copies[4])
+    value_grad(3, wait_sum, (1,))
+    key_grad(1, wait_sum, (2,))
+    key_grad(0, home, (0,))
+    value_grad(0, home, (1,))
+    ready_round(6)
 
     for copy in state_copies[2:]:
-        copy.wait_recv()
+        receive(copy)
     sums = jnp.zeros((ROWS, DH), F32)
     lane_at = lax.broadcasted_iota(jnp.int32, (ROWS, DH), 1)
     for h in range(PER_GROUP):
@@ -364,8 +452,32 @@
     for copy in x_copies:
         copy.start()
 
-    grad_copies[2].wait_recv()
-    grad_copies[3].wait_recv()
+    receive(grad_copies[1])
+    part[2, 1] = (wait_sum[1] + half[1].astype(F32)).astype(BF16)
+    start(grad_copies[5])
+    receive(grad_copies[0])
+    part[0, 0] = (wait_sum[2] + half[0].astype(F32)).astype(BF16)
+    start(grad_copies[6])
+
+    for copy in x_copies:
+        copy.wait_recv()
+    row_total = tot_x[0]
+    tail = jnp.zeros((8, DH), F32)
+    for k in range(1, X_RING):
+        row_total = row_total + tot_x[k]
+        tail = tail + jnp.where(lax.rem(x - k + X_RING, X_RING) > x, tot_x[k], 0.0)
+    tot_z[0] = row_total
+    z_copies = [
+        transfer((tz_s, tz_r), k, tot_z.at[0], tot_z.at[k], (z_peer(-k), g), z_has(-k), z_has(k))
+        for k in range(1, z_ring)
+    ]
+    if z_ring > 2:
+        pl.when(z >= z_ring - 1)(lambda: pl.semaphore_wait(ready.at[z_ring - 2], 1))
+    for copy in z_copies:
+        start(copy)
+
+    for n in (3, 4, 5, 6):
+        receive(grad_copies[n])
     for m in range(2):
         total = home[m] + back[0, m].astype(F32) + back[1, m].astype(F32)
         final[m] = total.astype(BF16)
@@ -383,34 +495,35 @@
         :, pl.ds(pl.multiple_of(g * slot_rows, slot_rows), slot_rows), :
     ]
 
-    for copy in x_copies:
-        copy.wait_recv()
-    row_total = tot_x[0]
-    tail = jnp.zeros((8, DH), F32)
-    for k in range(1, X_RING):
-        row_total = row_total + tot_x[k]
-        tail = tail + jnp.where(lax.rem(x - k + X_RING, X_RING) > x, tot_x[k], 0.0)
-    tot_z[0] = row_total
-    z_copies = [
-        send(tot_z.at[0], tot_z.at[k], tz_s.at[k], tz_r.at[k], (z_peer(k), g))
-        for k in range(1, z_ring)
-    ]
     for copy in z_copies:
-        copy.start()
-    for copy in z_copies:
-        copy.wait_recv()
+        receive(copy)
     for k in range(1, z_ring):
-        tail = tail + jnp.where(lax.rem(z - k + z_ring, z_ring) > z, tot_z[k], 0.0)
+        tail = tail + jnp.where(z_has(k), tot_z[k], 0.0)
     dg[...] = (cum_row[0:8, :] + tail[:, 0:1])[0:PER_GROUP]
 
     for copy in final_copies:
         copy.wait_recv()
     gk[...] = landed[0]
     gv[...] = landed[1]
-    for copy in (
-        head_copies + kv_copies + state_copies + grad_copies + final_copies + x_copies + z_copies
-    ):
+    for copy in head_copies + x_copies + final_copies:
         copy.wait_send()
+    for copy in kv_copies + state_copies + grad_copies + z_copies:
+        sent(copy)
+
+
+def write_out(*refs):
+    count = 7
+    sources, targets, held = refs[:count], refs[count : 2 * count], refs[2 * count : 3 * count]
+    sem_in, sem_out = refs[3 * count :]
+    loads = [pltpu.make_async_copy(sources[n], held[n], sem_in.at[n]) for n in range(count)]
+    stores = [pltpu.make_async_copy(held[n], targets[n], sem_out.at[n]) for n in range(count)]
+    for load in loads:
+        load.start()
+    for load, store in zip(loads, stores):
+        load.wait()
+        store.start()
+    for store in stores:
+        store.wait()
 
 
 def on_device(
@@ -424,8 +537,9 @@
     vmem = pl.BlockSpec(memory_space=pltpu.VMEM)
     slot_rows, all_heads = cache_keys.shape
     dma = pltpu.SemaphoreType.DMA
+    any_space = pl.BlockSpec(memory_space=pl.ANY)
     heads_wide = pltpu.VMEM((PER_GROUP, ROWS, DH), F32)
-    return pl.pallas_call(
+    results = pl.pallas_call(
         lambda *refs: body(n_ctx, n_head, *refs),
         out_shape=(
             wide, cache, cache, wide, wide, wide, jax.ShapeDtypeStruct(log_decay.shape, F32),
@@ -440,9 +554,10 @@
             pltpu.VMEM((3, STATE_ROWS, DH), F32),
             pltpu.VMEM((3, STATE_ROWS, DH), F32),
             pltpu.VMEM((3, 2, ROWS, DH), BF16),
-            pltpu.VMEM((2, ROWS, DH), BF16),
+            pltpu.VMEM((3, ROWS, DH), BF16),
             pltpu.VMEM((2, 2, ROWS, DH), BF16),
             pltpu.VMEM((2, ROWS, DH), F32),
+            pltpu.VMEM((3, ROWS, DH), F32),
             pltpu.VMEM((2, ROWS, DH), BF16),
             pltpu.VMEM((2, slot_rows, all_heads), BF16),
             pltpu.VMEM((X_RING, 8, DH), F32),
@@ -463,8 +578,9 @@
             heads_wide,
             heads_wide,
             pltpu.VMEM((16, ROWS), F32),
-            dma((8,)), dma((8,)), dma((4,)), dma((4,)), dma((6,)), dma((6,)), dma((4,)), dma((4,)),
+            dma((8,)), dma((8,)), dma((7,)), dma((7,)), dma((6,)), dma((6,)), dma((7,)), dma((7,)),
             dma((8,)), dma((8,)), dma((4,)), dma((4,)), dma((8,)), dma((8,)),
+            pltpu.SemaphoreType.REGULAR((8,)),
         ],
         compiler_params=pltpu.CompilerParams(
             collective_id=0, has_side_effects=True, vmem_limit_bytes=56 * 1024 * 1024
@@ -473,6 +589,13 @@
         cross_query, cross_grad, cache_keys, cache_values, retention_query, retention_key,
         retention_value, retention_grad, log_decay, doc_offsets.reshape(1, -1),
     )
+    return pl.pallas_call(
+        write_out,
+        out_shape=tuple(jax.ShapeDtypeStruct(r.shape, r.dtype) for r in results),
+        in_specs=[any_space] * 7,
+        out_specs=(any_space,) * 7,
+        scratch_shapes=[pltpu.VMEM(r.shape, r.dtype) for r in results] + [dma((7,)), dma((7,))],
+    )(*results)
 
 
 def solution(mesh):

time: 82.5 us -> 69.3 us (0.84)
  the two profiles are of different devices: /device:TPU:3 before, /device:TPU:103 now
where the time goes in v3:
time: 69.3 us; the launch traced here: 69.2 us
  Pallas kernels  68.5 us (99%)
    pallas_call x1, Pallas kernels, on_device(): pl.pallas_call(lambda *refs: body(n_ctx, n_head, *refs), out_shape=(wide,...  66.2 us
    pallas_call x1, Pallas kernels, on_device(): pl.pallas_call(write_out, out_shape=tuple((jax.ShapeDtypeStruct(r.shape,...  2.35 us

profile of v3, /device:TPU:103, one launch (start us, length us, event | category | flops | bytes accessed | tf_op | source)
XLA Modules:
  0.0 69.2 jit_solution(2982891742735639364)
XLA Ops:
  0.6 66.2 %shard_map.153 = (bf16[512,384]{1,0:T(8,128)(2,1)}, bf16[64,1024]{1,0:T(8,128)(2,1)}, bf16[64,1024]{1,0:T(8,128)(2,1)}, bf16[512,384]{1,0:T(8,128)(2,1)}, bf16[5...) custom-call(bf16[512,384]{1,0:T(8,128)(2,1)} %refs_0_.1, bf16[512,384]{1,0:T(8,128)(2,1)} %refs_1_.1, ...), custom_call_target="tpu_custom_call" | custom-call | tf_op jit(solution)/shard_map/pallas_call | solution.py:542
  66.8 2.3 %shard_map.154 = (bf16[512,384]{1,0:T(8,128)(2,1)}, bf16[64,1024]{1,0:T(8,128)(2,1)}, bf16[64,1024]{1,0:T(8,128)(2,1)}, bf16[512,384]{1,0:T(8,128)(2,1)}, bf16[5...) custom-call(bf16[512,384]{1,0:T(8,128)(2,1)} %get-tuple-element.14.refs_0_, ...), custom_call_target="tpu_custom_call" | custom-call | tf_op jit(solution)/shard_map/pallas_call | solution.py:592

commit v4 on v3

--- a/solution.py
+++ b/solution.py
@@ -12,6 +12,8 @@
 ROWS = 512
 TILE = 256
 TILES = ROWS // TILE
+DOC_BLOCKS = 4
+STRIP = 128
 X_RING = 4
 SCALING = DH ** (-0.5)
 EXPONENT_SCALE = SCALING * 1.4426950408889634
@@ -50,8 +52,8 @@
     n_ctx, n_head,
     cq, cg, ck, cv, rq, rk, rv, rg, ld, offs,
     gq, gk, gv, oq, ok, ov, dg,
-    kvs, kvb, own_f, own_b, got_f, got_b, part, half, back, home, wait_sum, final, landed, tot_x, tot_z,
-    qs, os, kt, score, dprob, prob_t, dscore_t,
+    kvs, kvb, kv_thru, own_f, own_b, got_f, got_b, thru, part, half, back, grad_thru, home, wait_sum, final, landed, tot_x, tot_z,
+    qs, os, kt, score, dprob, tops, prob_t, dscore_t,
     start_row, cum_row, cum_col, last_w, first_w, qf, kf, vf, pad16,
     head_s, head_r, kv_s, kv_r, st_s, st_r, gr_s, gr_r, fin_s, fin_r, tx_s, tx_r, tz_s, tz_r, ready,
 ):
@@ -215,27 +217,38 @@
         return send(src, dst, sems[0].at[n], sems[1].at[n], device), sends, receives
 
     kv_sems, st_sems, gr_sems = (kv_s, kv_r), (st_s, st_r), (gr_s, gr_r)
+    over = (ctx_at(4), g)
+    inner, outer = (c >= 1) & (x > 0), x == 0
     kv_copies = [
-        transfer(kv_sems, 0, kvb.at[0, 0], kvb.at[1, 0], up, has(1), has(-1)),
+        transfer(kv_sems, 0, kvb.at[0, 0], kvb.at[1, 0], up, has(1) & (x < 3), inner),
         transfer(kv_sems, 1, kvb.at[0, 1], kvb.at[3, 1], far_up, has(3), has(-3)),
-        transfer(kv_sems, 2, kvb.at[0, 1], kvb.at[1, 1], up, has(1), has(-1)),
+        transfer(kv_sems, 2, kvb.at[0, 1], kvb.at[1, 1], up, has(1) & (x < 3), inner),
         transfer(kv_sems, 3, kvb.at[0, 0], kvb.at[3, 0], far_up, has(3), has(-3)),
-        transfer(kv_sems, 4, kvb.at[1, 0], kvb.at[2, 0], up, has(1) & has(-1), has(-2)),
+        transfer(kv_sems, 4, kvb.at[1, 0], kvb.at[2, 0], up, has(1) & inner, has(-2)),
         transfer(
             kv_sems, 5, kvb.at[3, 1], kvb.at[2, 1], down, has(-3), (c >= 2) & (c < n_ctx - 1)
         ),
         transfer(kv_sems, 6, kvb.at[1, 1], kvb.at[2, 1], up, c == n_ctx - 2, c == n_ctx - 1),
+        transfer(kv_sems, 7, kvb.at[0, 0], kv_thru.at[0], far_down, (x == 3) & has(1), outer & has(4)),
+        transfer(kv_sems, 8, kvb.at[0, 1], kv_thru.at[1], far_down, (x == 3) & has(1), outer & has(4)),
+        transfer(kv_sems, 9, kv_thru.at[0], kvb.at[1, 0], over, outer & has(4), outer & has(-4)),
+        transfer(kv_sems, 10, kv_thru.at[1], kvb.at[1, 1], over, outer & has(4), outer & has(-4)),
+        transfer(kv_sems, 4, kvb.at[1, 0], kvb.at[2, 0], up, outer & has(1) & has(-4), has(-2)),
     ]
     state_copies = [
-        transfer(st_sems, 0, own_f, got_f.at[0], up, has(1), has(-1)),
+        transfer(st_sems, 0, own_f, got_f.at[0], up, has(1) & (x < 3), has(-1) & (x > 0)),
         transfer(st_sems, 1, own_b, got_b.at[0], down, has(-1), has(1)),
-        transfer(st_sems, 2, own_f, got_f.at[2], far_up, has(3), has(-3)),
+        transfer(st_sems, 2, own_f, got_f.at[2], far_up, has(3) & (x < 3), has(-3) & (x != 2)),
         transfer(st_sems, 3, own_b, got_b.at[2], far_down, has(-3), has(3)),
         transfer(st_sems, 4, got_f.at[0], got_f.at[1], up, has(1) & has(-1), has(-2)),
         transfer(st_sems, 5, got_b.at[0], got_b.at[1], down, has(1) & has(-1), has(2)),
+        transfer(st_sems, 6, own_f, thru, far_down, (x == 3) & has(1), (x == 0) & has(4)),
+        transfer(st_sems, 7, own_f, thru, down, (x == 3) & has(3), (x == 2) & has(4)),
+        transfer(st_sems, 8, thru, got_f.at[0], over, (x == 0) & has(4), (x == 0) & has(-4)),
+        transfer(st_sems, 9, thru, got_f.at[2], over, (x == 2) & has(4), (x == 2) & has(-4)),
     ]
-    for copy in kv_copies[:4]:
-        start(copy)
+    for n in (7, 0, 1, 8, 2, 3):
+        start(kv_copies[n])
     ready_round(2)
 
     for i in range(TILES):
@@ -282,82 +295,128 @@
 
     lax.fori_loop(0, PER_GROUP, retention_head, 0)
 
+    def tile_strips(i):
+        strips = []
+        for d in range(DOC_BLOCKS):
+            first, stop = (0, (i + 1) * TILE) if d == 0 else (0, ROWS)
+            if d == DOC_BLOCKS - 1:
+                first = i * TILE
+            strips += [(d, at) for at in range(first, stop, STRIP)]
+        return strips
+
+    def tile_columns(h, i):
+        return pl.ds(pl.multiple_of(i * (PER_GROUP * TILE) + h * TILE, TILE), TILE)
+
+    def scores_of_block(block):
+        def one_head(h, nothing):
+            for i in range(TILES):
+                at_tile = h * TILES + i
+                cols = tile_columns(h, i)
+                query = qs[cols, :]
+                upstream = os[cols, :]
+                start_t = start_row[0:1, i * TILE : (i + 1) * TILE]
+                top = jnp.full((8, TILE), -1e30, F32) if block == 0 else tops[at_tile]
+                for n, (d, at_s) in enumerate(tile_strips(i)):
+                    if d != block:
+                        continue
+                    s = slice(at_s, at_s + STRIP)
+                    at = slice(n * STRIP, (n + 1) * STRIP)
+                    raw = matmul_nt(kvb[d, 0, s, :], query)
+                    allowed = strip_pos >= start_t + float(d * ROWS - at_s)
+                    if d == 0 and at_s >= i * TILE:
+                        allowed = allowed & (strip_row + (at_s - i * TILE) <= strip_col)
+                    raw = jnp.where(allowed, raw, -1e30)
+                    score[at_tile, at, :] = raw
+                    top = jnp.maximum(top, jnp.max(raw.reshape(STRIP // 8, 8, TILE), axis=0))
+                    dprob[at_tile, at, :] = matmul_nt(kvb[d, 1, s, :], upstream)
+                tops[at_tile] = top
+            return nothing
+
+        lax.fori_loop(0, PER_GROUP, one_head, 0)
+
+    strip_row = lax.broadcasted_iota(jnp.int32, (STRIP, TILE), 0)
+    strip_col = lax.broadcasted_iota(jnp.int32, (STRIP, TILE), 1)
+    strip_pos = strip_row.astype(F32)
+
+    receive(kv_copies[7])
+    start(kv_copies[9])
     for n in (0, 1):
         receive(kv_copies[n])
-    start(kv_copies[4])
-    start(kv_copies[5])
+        start(kv_copies[n + 4])
+    for n in (6, 7, 1, 0, 3, 2):
+        start(state_copies[n])
+    scores_of_block(0)
+    receive(kv_copies[8])
+    start(kv_copies[10])
     receive(kv_copies[2])
     start(kv_copies[6])
     receive(kv_copies[3])
     ready_round(3)
+    scores_of_block(3)
+    receive(kv_copies[9])
+    start(kv_copies[11])
+    receive(kv_copies[10])
+    scores_of_block(1)
+    for n in (6, 7):
+        receive(state_copies[n])
+        start(state_copies[n + 2])
     for d in (0, 1, 3):
         kt[d] = kvb[d, 0].astype(F32).T.astype(BF16)
     for n in (4, 5, 6):
         receive(kv_copies[n])
     kt[2] = kvb[2, 0].astype(F32).T.astype(BF16)
-    start(state_copies[0])
-    start(state_copies[1])
+    receive(state_copies[1])
+    start(state_copies[5])
+    scores_of_block(2)
+    receive(state_copies[0])
+    receive(state_copies[8])
+    start(state_copies[4])
 
     def attention_head(h, nothing):
         for i in range(TILES):
-            cols = pl.ds(pl.multiple_of(i * (PER_GROUP * TILE) + h * TILE, TILE), TILE)
-            query = qs[cols, :]
-            upstream = os[cols, :]
-            start_t = start_row[0:1, i * TILE : (i + 1) * TILE]
-            pieces = [(0, j) for j in range(i + 1)]
-            pieces += [(d, j) for d in (1, 2) for j in range(TILES)]
-            pieces += [(3, j) for j in range(i, TILES)]
-            top = jnp.full((1, TILE), -1e30, F32)
-            for n, (d, j) in enumerate(pieces):
-                s = slice(j * TILE, (j + 1) * TILE)
-                raw = matmul_nt(kvb[d, 0, s, :], query)
-                allowed = tile_pos >= start_t + float(d * ROWS - j * TILE)
-                if d == 0 and j == i:
-                    allowed = allowed & causal
-                raw = jnp.where(allowed, raw, -1e30)
-                score[n * TILE : (n + 1) * TILE, :] = raw
-                top = jnp.maximum(top, jnp.max(raw, axis=0, keepdims=True))
-            total = jnp.zeros((1, TILE), F32)
-            for n in range(len(pieces)):
-                at = slice(n * TILE, (n + 1) * TILE)
-                term = jnp.exp2((score[at, :] - top) * EXPONENT_SCALE)
-                score[at, :] = term
-                total = total + jnp.sum(term, axis=0, keepdims=True)
-            inverse = 1.0 / total
-            row_dot = jnp.zeros((1, TILE), F32)
-            for n, (d, j) in enumerate(pieces):
-                s = slice(j * TILE, (j + 1) * TILE)
-                at = slice(n * TILE, (n + 1) * TILE)
-                weights = score[at, :] * inverse
+            at_tile = h * TILES + i
+            cols = tile_columns(h, i)
+            strips = tile_strips(i)
+            top = jnp.max(tops[at_tile], axis=0, keepdims=True)
+            total = jnp.zeros((8, TILE), F32)
+            for n in range(len(strips)):
+                at = slice(n * STRIP, (n + 1) * STRIP)
+                term = jnp.exp2((score[at_tile, at, :] - top) * EXPONENT_SCALE)
+                score[at_tile, at, :] = term
+                total = total + jnp.sum(term.reshape(STRIP // 8, 8, TILE), axis=0)
+            inverse = 1.0 / jnp.sum(total, axis=0, keepdims=True)
+            row_dot = jnp.zeros((8, TILE), F32)
+            for n, (d, at_s) in enumerate(strips):
+                s = slice(at_s, at_s + STRIP)
+                at = slice(n * STRIP, (n + 1) * STRIP)
+                weights = score[at_tile, at, :] * inverse
                 weights_b = weights.astype(BF16)
-                dweights = matmul_nt(kvb[d, 1, s, :], upstream)
-                score[at, :] = weights
-                dprob[at, :] = dweights
                 prob_t[d, s, cols] = weights_b
-                row_dot = row_dot + jnp.sum(weights_b.astype(F32) * dweights, axis=0, keepdims=True)
+                products = weights_b.astype(F32) * dprob[at_tile, at, :]
+                row_dot = row_dot + jnp.sum(products.reshape(STRIP // 8, 8, TILE), axis=0)
+            row_dot = jnp.sum(row_dot, axis=0, keepdims=True)
             query_t = jnp.zeros((DH, TILE), F32)
-            for n, (d, j) in enumerate(pieces):
-                s = slice(j * TILE, (j + 1) * TILE)
-                at = slice(n * TILE, (n + 1) * TILE)
-                dscores_b = (score[at, :] * (dprob[at, :] - row_dot)).astype(BF16)
+            for n, (d, at_s) in enumerate(strips):
+                s = slice(at_s, at_s + STRIP)
+                at = slice(n * STRIP, (n + 1) * STRIP)
+                gaps = dprob[at_tile, at, :] - row_dot
+                dscores_b = ((score[at_tile, at, :] * inverse) * gaps).astype(BF16)
                 dscore_t[d, s, cols] = dscores_b
-                query_t = query_t + matmul(kt[d, :, s], dscores_b)
+            for d in range(DOC_BLOCKS):
+                first, stop = (0, (i + 1) * TILE) if d == 0 else (0, ROWS)
+                if d == DOC_BLOCKS - 1:
+                    first = i * TILE
+                query_t = query_t + matmul(kt[d, :, first:stop], dscore_t[d, first:stop, cols])
             gq[i * TILE : (i + 1) * TILE, pl.ds(pl.multiple_of(h * DH, DH), DH)] = (
                 query_t.T * SCALING
             ).astype(BF16)
 
         @pl.when(h == 0)
         def _():
-            start(state_copies[2])
-            start(state_copies[3])
             ready_round(4)
 
         @pl.when(h == 1)
         def _():
-            receive(state_copies[0])
-            start(state_copies[4])
-            receive(state_copies[1])
-            start(state_copies[5])
             ready_round(5)
 
         return nothing
@@ -380,9 +439,15 @@
         transfer(gr_sems, 1, part.at[1, 1], half.at[1], up, has(-2) & has(1), has(-3)),
         transfer(gr_sems, 2, part.at[1, 1], half.at[2], down, c == n_ctx - 1, c == n_ctx - 2),
         transfer(gr_sems, 3, part.at[2, 0], back.at[1, 0], far_down, has(-3), has(3)),
-        transfer(gr_sems, 4, part.at[0, 1], back.at[0, 1], down, has(-1), has(1)),
+        transfer(
+            gr_sems, 4, part.at[0, 1], back.at[0, 1], down, has(-1) & (x > 0), has(1) & (x < 3)
+        ),
         transfer(gr_sems, 5, part.at[2, 1], back.at[1, 1], far_down, has(-3), has(3)),
         transfer(gr_sems, 6, part.at[0, 0], back.at[0, 0], down, has(-1), has(1)),
+        transfer(gr_sems, 7, part.at[0, 1], grad_thru, far_up, (x == 0) & has(-4), (x == 3) & has(-4)),
+        transfer(
+            gr_sems, 8, grad_thru, back.at[0, 1], (ctx_at(-4), g), (x == 3) & has(-4), (x == 3) & has(4)
+        ),
     ]
 
     def key_grad(d, out, at):
@@ -410,14 +475,15 @@
 
     part[0, 1] = (wait_sum[0] + half[2].astype(F32)).astype(BF16)
     start(grad_copies[4])
+    start(grad_copies[7])
     value_grad(3, wait_sum, (1,))
     key_grad(1, wait_sum, (2,))
     key_grad(0, home, (0,))
     value_grad(0, home, (1,))
     ready_round(6)
 
-    for copy in state_copies[2:]:
-        receive(copy)
+    for n in (2, 3, 4, 5, 9):
+        receive(state_copies[n])
     sums = jnp.zeros((ROWS, DH), F32)
     lane_at = lax.broadcasted_iota(jnp.int32, (ROWS, DH), 1)
     for h in range(PER_GROUP):
@@ -452,6 +518,8 @@
     for copy in x_copies:
         copy.start()
 
+    receive(grad_copies[7])
+    start(grad_copies[8])
     receive(grad_copies[1])
     part[2, 1] = (wait_sum[1] + half[1].astype(F32)).astype(BF16)
     start(grad_copies[5])
@@ -476,7 +544,7 @@
     for copy in z_copies:
         start(copy)
 
-    for n in (3, 4, 5, 6):
+    for n in (3, 4, 5, 6, 8):
         receive(grad_copies[n])
     for m in range(2):
         total = home[m] + back[0, m].astype(F32) + back[1, m].astype(F32)
@@ -549,13 +617,16 @@
         scratch_shapes=[
             pltpu.VMEM((2, slot_rows, all_heads), BF16),
             pltpu.VMEM((4, 2, ROWS, DH), BF16),
+            pltpu.VMEM((2, ROWS, DH), BF16),
             pltpu.VMEM((STATE_ROWS, DH), F32),
             pltpu.VMEM((STATE_ROWS, DH), F32),
             pltpu.VMEM((3, STATE_ROWS, DH), F32),
             pltpu.VMEM((3, STATE_ROWS, DH), F32),
+            pltpu.VMEM((STATE_ROWS, DH), F32),
             pltpu.VMEM((3, 2, ROWS, DH), BF16),
             pltpu.VMEM((3, ROWS, DH), BF16),
             pltpu.VMEM((2, 2, ROWS, DH), BF16),
+            pltpu.VMEM((ROWS, DH), BF16),
             pltpu.VMEM((2, ROWS, DH), F32),
             pltpu.VMEM((3, ROWS, DH), F32),
             pltpu.VMEM((2, ROWS, DH), BF16),
@@ -565,8 +636,9 @@
             pltpu.VMEM((PER_GROUP * ROWS, DH), BF16),
             pltpu.VMEM((PER_GROUP * ROWS, DH), BF16),
             pltpu.VMEM((4, DH, ROWS), BF16),
-            pltpu.VMEM((7 * TILE, TILE), F32),
-            pltpu.VMEM((7 * TILE, TILE), F32),
+            pltpu.VMEM((PER_GROUP * TILES, 7 * TILE, TILE), F32),
+            pltpu.VMEM((PER_GROUP * TILES, 7 * TILE, TILE), F32),
+            pltpu.VMEM((PER_GROUP * TILES, 8, TILE), F32),
             pltpu.VMEM((4, ROWS, PER_GROUP * ROWS), BF16),
             pltpu.VMEM((4, ROWS, PER_GROUP * ROWS), BF16),
             pltpu.VMEM((8, ROWS), F32),
@@ -578,7 +650,7 @@
             heads_wide,
             heads_wide,
             pltpu.VMEM((16, ROWS), F32),
-            dma((8,)), dma((8,)), dma((7,)), dma((7,)), dma((6,)), dma((6,)), dma((7,)), dma((7,)),
+            dma((8,)), dma((8,)), dma((11,)), dma((11,)), dma((10,)), dma((10,)), dma((9,)), dma((9,)),
             dma((8,)), dma((8,)), dma((4,)), dma((4,)), dma((8,)), dma((8,)),
             pltpu.SemaphoreType.REGULAR((8,)),
         ],

time: 69.3 us -> 66.3 us (0.957)
  Pallas kernels: 68.5 us -> 65.5 us
    pallas_call x1, Pallas kernels: 66.2 us -> 63.1 us  [on_device(): pl.pallas_call(lambda *refs: body(n_ctx, n_head, *refs), out_shape=(wide,...]
where the time goes in v4:
time: 66.3 us; the launch traced here: 66.1 us
  Pallas kernels  65.5 us (99%)
    pallas_call x1, Pallas kernels, on_device(): pl.pallas_call(lambda *refs: body(n_ctx, n_head, *refs), out_shape=(wide,...  63.1 us
    pallas_call x1, Pallas kernels, on_device(): pl.pallas_call(write_out, out_shape=tuple((jax.ShapeDtypeStruct(r.shape,...  2.35 us

profile of v4, /device:TPU:103, one launch (start us, length us, event | category | flops | bytes accessed | tf_op | source)
XLA Modules:
  0.0 66.1 jit_solution(6833617354831627138)
XLA Ops:
  0.6 63.1 %shard_map.153 = (bf16[512,384]{1,0:T(8,128)(2,1)}, bf16[64,1024]{1,0:T(8,128)(2,1)}, bf16[64,1024]{1,0:T(8,128)(2,1)}, bf16[512,384]{1,0:T(8,128)(2,1)}, bf16[5...) custom-call(bf16[512,384]{1,0:T(8,128)(2,1)} %refs_0_.1, bf16[512,384]{1,0:T(8,128)(2,1)} %refs_1_.1, ...), custom_call_target="tpu_custom_call" | custom-call | tf_op jit(solution)/shard_map/pallas_call | solution.py:610
  63.8 2.3 %shard_map.154 = (bf16[512,384]{1,0:T(8,128)(2,1)}, bf16[64,1024]{1,0:T(8,128)(2,1)}, bf16[64,1024]{1,0:T(8,128)(2,1)}, bf16[512,384]{1,0:T(8,128)(2,1)}, bf16[5...) custom-call(bf16[512,384]{1,0:T(8,128)(2,1)} %get-tuple-element.14.refs_0_, ...), custom_call_target="tpu_custom_call" | custom-call | tf_op jit(solution)/shard_map/pallas_call | solution.py:664

commit v5 on v4

--- a/solution.py
+++ b/solution.py
@@ -50,8 +50,9 @@
 
 def body(
     n_ctx, n_head,
-    cq, cg, ck, cv, rq, rk, rv, rg, ld, offs,
-    gq, gk, gv, oq, ok, ov, dg,
+    cq, cg, ck, cv, rq_in, rk_in, rv_in, rg_in, ld, offs,
+    gq_out, gk, gv, oq_out, ok_out, ov_out, dg,
+    rq, rk, rv, rg, gq, oq, ok, ov, in_sem, tile_sem, out_sem,
     kvs, kvb, kv_thru, own_f, own_b, got_f, got_b, thru, part, half, back, grad_thru, home, wait_sum, final, landed, tot_x, tot_z,
     qs, os, kt, score, dprob, tops, prob_t, dscore_t,
     start_row, cum_row, cum_col, last_w, first_w, qf, kf, vf, pad16,
@@ -137,6 +138,20 @@
                 pl.semaphore_signal(
                     ready.at[r], inc=1, device_id=(z_peer(1), g), device_id_type=MESH
                 )
+
+    loads = [
+        pltpu.make_async_copy(source, held, in_sem.at[n])
+        for n, (source, held) in enumerate(((rq_in, rq), (rk_in, rk), (rv_in, rv), (rg_in, rg)))
+    ]
+    for i in range(TILES):
+        for h in range(PER_GROUP):
+            rows = pl.ds((i * PER_GROUP + h) * TILE, TILE)
+            block = (pl.ds(i * TILE, TILE), pl.ds(h * DH, DH))
+            n = 2 * (i * PER_GROUP + h)
+            loads.append(pltpu.make_async_copy(cq.at[block], qs.at[rows, :], tile_sem.at[n]))
+            loads.append(pltpu.make_async_copy(cg.at[block], os.at[rows, :], tile_sem.at[n + 1]))
+    for load in loads:
+        load.start()
 
     for d in (1, 2, 3):
         clear(c < d, kvb.at[d])
@@ -183,6 +198,8 @@
 
     ready_round(1)
 
+    for load in loads[:4]:
+        load.wait()
     carry_rows = []
     for h in range(PER_GROUP):
         lanes = slice(h * DH, (h + 1) * DH)
@@ -219,21 +236,44 @@
     kv_sems, st_sems, gr_sems = (kv_s, kv_r), (st_s, st_r), (gr_s, gr_r)
     over = (ctx_at(4), g)
     inner, outer = (c >= 1) & (x > 0), x == 0
+    upper, lower = pl.ds(0, TILE), pl.ds(TILE, TILE)
     kv_copies = [
         transfer(kv_sems, 0, kvb.at[0, 0], kvb.at[1, 0], up, has(1) & (x < 3), inner),
         transfer(kv_sems, 1, kvb.at[0, 1], kvb.at[3, 1], far_up, has(3), has(-3)),
         transfer(kv_sems, 2, kvb.at[0, 1], kvb.at[1, 1], up, has(1) & (x < 3), inner),
         transfer(kv_sems, 3, kvb.at[0, 0], kvb.at[3, 0], far_up, has(3), has(-3)),
-        transfer(kv_sems, 4, kvb.at[1, 0], kvb.at[2, 0], up, has(1) & inner, has(-2)),
+        transfer(kv_sems, 4, kvb.at[1, 0, upper], kvb.at[2, 0, upper], up, has(1) & inner, has(-2)),
         transfer(
             kv_sems, 5, kvb.at[3, 1], kvb.at[2, 1], down, has(-3), (c >= 2) & (c < n_ctx - 1)
         ),
         transfer(kv_sems, 6, kvb.at[1, 1], kvb.at[2, 1], up, c == n_ctx - 2, c == n_ctx - 1),
-        transfer(kv_sems, 7, kvb.at[0, 0], kv_thru.at[0], far_down, (x == 3) & has(1), outer & has(4)),
+        transfer(
+            kv_sems, 7, kvb.at[0, 0, upper], kv_thru.at[0, upper], far_down,
+            (x == 3) & has(1), outer & has(4),
+        ),
         transfer(kv_sems, 8, kvb.at[0, 1], kv_thru.at[1], far_down, (x == 3) & has(1), outer & has(4)),
-        transfer(kv_sems, 9, kv_thru.at[0], kvb.at[1, 0], over, outer & has(4), outer & has(-4)),
+        transfer(
+            kv_sems, 9, kv_thru.at[0, upper], kvb.at[1, 0, upper], over,
+            outer & has(4), outer & has(-4),
+        ),
         transfer(kv_sems, 10, kv_thru.at[1], kvb.at[1, 1], over, outer & has(4), outer & has(-4)),
-        transfer(kv_sems, 4, kvb.at[1, 0], kvb.at[2, 0], up, outer & has(1) & has(-4), has(-2)),
+        transfer(
+            kv_sems, 4, kvb.at[1, 0, upper], kvb.at[2, 0, upper], up,
+            outer & has(1) & has(-4), has(-2),
+        ),
+        transfer(kv_sems, 11, kvb.at[1, 0, lower], kvb.at[2, 0, lower], up, has(1) & inner, has(-2)),
+        transfer(
+            kv_sems, 12, kvb.at[0, 0, lower], kv_thru.at[0, lower], far_down,
+            (x == 3) & has(1), outer & has(4),
+        ),
+        transfer(
+            kv_sems, 13, kv_thru.at[0, lower], kvb.at[1, 0, lower], over,
+            outer & has(4), outer & has(-4),
+        ),
+        transfer(
+            kv_sems, 11, kvb.at[1, 0, lower], kvb.at[2, 0, lower], up,
+            outer & has(1) & has(-4), has(-2),
+        ),
     ]
     state_copies = [
         transfer(st_sems, 0, own_f, got_f.at[0], up, has(1) & (x < 3), has(-1) & (x > 0)),
@@ -247,15 +287,12 @@
         transfer(st_sems, 8, thru, got_f.at[0], over, (x == 0) & has(4), (x == 0) & has(-4)),
         transfer(st_sems, 9, thru, got_f.at[2], over, (x == 2) & has(4), (x == 2) & has(-4)),
     ]
-    for n in (7, 0, 1, 8, 2, 3):
+    for n in (7, 13, 0, 1, 8, 2, 3):
         start(kv_copies[n])
     ready_round(2)
 
-    for i in range(TILES):
-        for h in range(PER_GROUP):
-            at = (i * PER_GROUP + h) * TILE
-            qs[at : at + TILE, :] = cq[i * TILE : (i + 1) * TILE, h * DH : (h + 1) * DH]
-            os[at : at + TILE, :] = cg[i * TILE : (i + 1) * TILE, h * DH : (h + 1) * DH]
+    for load in loads[4:]:
+        load.wait()
 
     tile_row = lax.broadcasted_iota(jnp.int32, (TILE, TILE), 0)
     tile_col = lax.broadcasted_iota(jnp.int32, (TILE, TILE), 1)
@@ -321,7 +358,7 @@
                         continue
                     s = slice(at_s, at_s + STRIP)
                     at = slice(n * STRIP, (n + 1) * STRIP)
-                    raw = matmul_nt(kvb[d, 0, s, :], query)
+                    raw = matmul_nt(kvb[d, 0, s, :], query) * EXPONENT_SCALE
                     allowed = strip_pos >= start_t + float(d * ROWS - at_s)
                     if d == 0 and at_s >= i * TILE:
                         allowed = allowed & (strip_row + (at_s - i * TILE) <= strip_col)
@@ -340,21 +377,27 @@
 
     receive(kv_copies[7])
     start(kv_copies[9])
-    for n in (0, 1):
-        receive(kv_copies[n])
-        start(kv_copies[n + 4])
+    receive(kv_copies[13])
+    start(kv_copies[14])
+    receive(kv_copies[0])
+    start(kv_copies[4])
+    start(kv_copies[12])
+    receive(kv_copies[1])
+    start(kv_copies[5])
     for n in (6, 7, 1, 0, 3, 2):
         start(state_copies[n])
     scores_of_block(0)
+    receive(kv_copies[9])
+    start(kv_copies[11])
     receive(kv_copies[8])
     start(kv_copies[10])
+    receive(kv_copies[14])
+    start(kv_copies[15])
     receive(kv_copies[2])
     start(kv_copies[6])
     receive(kv_copies[3])
     ready_round(3)
     scores_of_block(3)
-    receive(kv_copies[9])
-    start(kv_copies[11])
     receive(kv_copies[10])
     scores_of_block(1)
     for n in (6, 7):
@@ -362,7 +405,7 @@
         start(state_copies[n + 2])
     for d in (0, 1, 3):
         kt[d] = kvb[d, 0].astype(F32).T.astype(BF16)
-    for n in (4, 5, 6):
+    for n in (4, 12, 5, 6):
         receive(kv_copies[n])
     kt[2] = kvb[2, 0].astype(F32).T.astype(BF16)
     receive(state_copies[1])
@@ -381,7 +424,7 @@
             total = jnp.zeros((8, TILE), F32)
             for n in range(len(strips)):
                 at = slice(n * STRIP, (n + 1) * STRIP)
-                term = jnp.exp2((score[at_tile, at, :] - top) * EXPONENT_SCALE)
+                term = jnp.exp2(score[at_tile, at, :] - top)
                 score[at_tile, at, :] = term
                 total = total + jnp.sum(term.reshape(STRIP // 8, 8, TILE), axis=0)
             inverse = 1.0 / jnp.sum(total, axis=0, keepdims=True)
@@ -423,6 +466,9 @@
 
     lax.fori_loop(0, PER_GROUP, attention_head, 0)
 
+    stores = [pltpu.make_async_copy(gq, gq_out, out_sem.at[0])]
+    stores[0].start()
+
     width = PER_GROUP * TILE
 
     def partial_at(d, j):
@@ -508,6 +554,9 @@
             rk[:, lanes].astype(F32) * key_f, axis=1, keepdims=True
         )
         sums = jnp.where(lane_at == h, residue, sums)
+    for n, (held, target) in enumerate(((oq, oq_out), (ok, ok_out), (ov, ov_out))):
+        stores.append(pltpu.make_async_copy(held, target, out_sem.at[n + 1]))
+        stores[-1].start()
     suffix = triangle_sum(sums.T[0:16], (row_at >= col_at).astype(F32).astype(BF16))
     cum_row[...] = suffix
     tot_x[0] = jnp.broadcast_to(suffix[0:8, 0:1], (8, DH))
@@ -571,8 +620,11 @@
 
     for copy in final_copies:
         copy.wait_recv()
-    gk[...] = landed[0]
-    gv[...] = landed[1]
+    for m, target in enumerate((gk, gv)):
+        stores.append(pltpu.make_async_copy(landed.at[m], target, out_sem.at[m + 4]))
+        stores[-1].start()
+    for store in stores:
+        store.wait()
     for copy in head_copies + x_copies + final_copies:
         copy.wait_send()
     for copy in kv_copies + state_copies + grad_copies + z_copies:
@@ -612,9 +664,11 @@
         out_shape=(
             wide, cache, cache, wide, wide, wide, jax.ShapeDtypeStruct(log_decay.shape, F32),
         ),
-        in_specs=[vmem] * 10,
-        out_specs=(vmem,) * 7,
+        in_specs=[any_space] * 2 + [vmem] * 2 + [any_space] * 4 + [vmem] * 2,
+        out_specs=(any_space,) * 6 + (vmem,),
         scratch_shapes=[
+            *[pltpu.VMEM(cross_query.shape, BF16)] * 8,
+            dma((4,)), dma((2 * PER_GROUP * TILES,)), dma((6,)),
             pltpu.VMEM((2, slot_rows, all_heads), BF16),
             pltpu.VMEM((4, 2, ROWS, DH), BF16),
             pltpu.VMEM((2, ROWS, DH), BF16),
@@ -650,7 +704,7 @@
             heads_wide,
             heads_wide,
             pltpu.VMEM((16, ROWS), F32),
-            dma((8,)), dma((8,)), dma((11,)), dma((11,)), dma((10,)), dma((10,)), dma((9,)), dma((9,)),
+            dma((8,)), dma((8,)), dma((14,)), dma((14,)), dma((10,)), dma((10,)), dma((9,)), dma((9,)),
             dma((8,)), dma((8,)), dma((4,)), dma((4,)), dma((8,)), dma((8,)),
             pltpu.SemaphoreType.REGULAR((8,)),
         ],

time: 66.3 us -> 64.5 us (0.973)
  Pallas kernels: 65.5 us -> 63.7 us
    pallas_call x1, Pallas kernels: 63.1 us -> 61.4 us  [on_device(): pl.pallas_call(lambda *refs: body(n_ctx, n_head, *refs), out_shape=(wide,...]
where the time goes in v5:
time: 64.5 us; the launch traced here: 64.4 us
  Pallas kernels  63.7 us (99%)
    pallas_call x1, Pallas kernels, on_device(): pl.pallas_call(lambda *refs: body(n_ctx, n_head, *refs), out_shape=(wide,...  61.4 us
    pallas_call x1, Pallas kernels, on_device(): pl.pallas_call(write_out, out_shape=tuple((jax.ShapeDtypeStruct(r.shape,...  2.35 us

profile of v5, /device:TPU:103, one launch (start us, length us, event | category | flops | bytes accessed | tf_op | source)
XLA Modules:
  0.0 64.4 jit_solution(12993051646424539627)
XLA Ops:
  0.6 61.4 %shard_map.153 = (bf16[512,384]{1,0:T(8,128)(2,1)}, bf16[64,1024]{1,0:T(8,128)(2,1)}, bf16[64,1024]{1,0:T(8,128)(2,1)}, bf16[512,384]{1,0:T(8,128)(2,1)}, bf16[5...) custom-call(bf16[512,384]{1,0:T(8,128)(2,1)} %refs_0_.1, bf16[512,384]{1,0:T(8,128)(2,1)} %refs_1_.1, ...), custom_call_target="tpu_custom_call" | custom-call | tf_op jit(solution)/shard_map/pallas_call | solution.py:662
  62.0 2.3 %shard_map.154 = (bf16[512,384]{1,0:T(8,128)(2,1)}, bf16[64,1024]{1,0:T(8,128)(2,1)}, bf16[64,1024]{1,0:T(8,128)(2,1)}, bf16[512,384]{1,0:T(8,128)(2,1)}, bf16[5...) custom-call(bf16[512,384]{1,0:T(8,128)(2,1)} %get-tuple-element.14.refs_0_, ...), custom_call_target="tpu_custom_call" | custom-call | tf_op jit(solution)/shard_map/pallas_call | solution.py:718

commit v6 on v5

--- a/solution.py
+++ b/solution.py
@@ -464,7 +464,7 @@
 
         return nothing
 
-    lax.fori_loop(0, PER_GROUP, attention_head, 0)
+    lax.fori_loop(0, PER_GROUP, attention_head, 0, unroll=True)
 
     stores = [pltpu.make_async_copy(gq, gq_out, out_sem.at[0])]
     stores[0].start()

time: 64.5 us -> 63.7 us (0.988)
  Pallas kernels: 63.7 us -> 62.7 us
    pallas_call x1, Pallas kernels: 61.4 us -> 60.3 us  [on_device(): pl.pallas_call(lambda *refs: body(n_ctx, n_head, *refs), out_shape=(wide,...]
where the time goes in v6:
time: 63.7 us; the launch traced here: 63.5 us
  Pallas kernels  62.7 us (98%)
  between operations  0.8 us (1%)
    pallas_call x1, Pallas kernels, on_device(): pl.pallas_call(lambda *refs: body(n_ctx, n_head, *refs), out_shape=(wide,...  60.3 us
    pallas_call x1, Pallas kernels, on_device(): pl.pallas_call(write_out, out_shape=tuple((jax.ShapeDtypeStruct(r.shape,...  2.35 us

profile of v6, /device:TPU:103, one launch (start us, length us, event | category | flops | bytes accessed | tf_op | source)
XLA Modules:
  0.0 63.5 jit_solution(12381996919243498897)
XLA Ops:
  0.6 60.3 %shard_map.153 = (bf16[512,384]{1,0:T(8,128)(2,1)}, bf16[64,1024]{1,0:T(8,128)(2,1)}, bf16[64,1024]{1,0:T(8,128)(2,1)}, bf16[512,384]{1,0:T(8,128)(2,1)}, bf16[5...) custom-call(bf16[512,384]{1,0:T(8,128)(2,1)} %refs_0_.1, bf16[512,384]{1,0:T(8,128)(2,1)} %refs_1_.1, ...), custom_call_target="tpu_custom_call" | custom-call | tf_op jit(solution)/shard_map/pallas_call | solution.py:662
  61.0 2.3 %shard_map.154 = (bf16[512,384]{1,0:T(8,128)(2,1)}, bf16[64,1024]{1,0:T(8,128)(2,1)}, bf16[64,1024]{1,0:T(8,128)(2,1)}, bf16[512,384]{1,0:T(8,128)(2,1)}, bf16[5...) custom-call(bf16[512,384]{1,0:T(8,128)(2,1)} %get-tuple-element.14.refs_0_, ...), custom_call_target="tpu_custom_call" | custom-call | tf_op jit(solution)/shard_map/pallas_call | solution.py:718
